TPU v7x, 512 devices: a whole 4x4x16 slice. The times are simulated.
512 devices in a mesh: heads: 8 (over x, core), frames: 64 (over y, z).
Axes of the slice: x: 4, y: 4, z: 16, core: 2. Of those that a mesh axis runs over, the one named last changes fastest.
Arguments:
- queries: bfloat16 [64, 512, 5120], P('frames', None, 'heads'), may hold values from -120 to 120
- keys: bfloat16 [64, 512, 5120], P('frames', None, 'heads'), may hold values from -120 to 120
- values: bfloat16 [64, 512, 5120], P('frames', None, 'heads'), may hold values from -6 to 6
- gain_q: float32 [5120], P('heads'), may hold values from 0.25 to 1.75
- gain_k: float32 [5120], P('heads'), may hold values from 0.25 to 1.75
- head_kind: int32 [40], P('heads'), may hold values from 0 to 1, as said below
- tile_mask: int32 [40, 4, 12], P('heads'), may hold values from 0 to 1, as said below
- frame_valid: int32 [64], replicated, may hold values from 0 to 1, as said below
Outputs:
- attended: bfloat16 [64, 512, 5120], P('frames', None, 'heads')
Inputs may be any that keep to these rules, and one draw needn't show every extreme that they name: `head_kind`: in each block of 5 consecutive heads, 1 to 4 heads are spatial; some block has 4 spatial heads and some block exactly one. tile_mask[h, i, 4 + i] = 1 for every head h and query tile i. Each video has a live count of more than 16 and less than 32; frame_valid is 1 exactly on the frames whose position in their video is below that count.
All inputs are finite; a program needn't handle non-finite values.
Results may differ from a plain program's by a relative error of at most 0.007.
Values may be sent and summed in bfloat16 or wider, within the bound.
No kernel may reach another device: no remote copies, remote signals or barrier semaphores. Data moves between devices by JAX's collectives and lax.ppermute only.
A program may use at most 64 MiB of HBM per device.

v0:
```python
import math

import jax
import jax.numpy as jnp
from jax import lax
from jax.sharding import PartitionSpec as P

epsilon = 1e-06


def padded(x, sides, width):
    for axis, dim in sides:
        size, length = (lax.axis_size(axis), x.shape[dim])
        up = [(i, (i + 1) % size) for i in range(size - 1)]
        down = [(j, i) for i, j in up]
        last = lax.slice_in_dim(x, length - width, length, axis=dim)
        initial = lax.slice_in_dim(x, 0, width, axis=dim)
        before = lax.ppermute(last, axis, up)
        after = lax.ppermute(initial, axis, down)
        x = jnp.concatenate([before, x, after], axis=dim)
    return x


def soft_attend(query_rows, key_rows, value_rows, allowed, score_scale):
    scores = (
        lax.dot_general(
            query_rows, key_rows, (((1,), (1,)), ((), ())), preferred_element_type=jnp.float32
        )
        * score_scale
    )
    scores = jnp.where(allowed, scores, -jnp.inf)
    row_max = jnp.max(scores, axis=1, keepdims=True)
    exp_terms = jnp.exp(scores - row_max)
    row_total = jnp.sum(exp_terms, axis=1, keepdims=True)
    weighted = jnp.dot(
        exp_terms.astype(jnp.bfloat16), value_rows, preferred_element_type=jnp.float32
    )
    return weighted / row_total


def local(queries, keys, values, gain_q, gain_k, head_kind, tile_mask, frame_valid):
    head_count = head_kind.shape[0]
    channels = queries.shape[2]
    head_size = channels // head_count
    tokens = queries.shape[1]
    tile_size = tokens // tile_mask.shape[1]
    frame_count = lax.axis_size("frames")
    video_frames = min(32, frame_count)
    frame_offset = (
        video_frames // 4 + video_frames * frame_count - frame_count // 2
    ) % video_frames
    position = lax.axis_index("frames")
    score_scale = 1.0 / math.sqrt(head_size)
    block_rows = min(tokens, 512)
    wide_q = queries.astype(jnp.float32)
    wide_k = keys.astype(jnp.float32)
    sums_q, sums_k = lax.psum(
        (
            jnp.sum(wide_q * wide_q, axis=2, keepdims=True),
            jnp.sum(wide_k * wide_k, axis=2, keepdims=True),
        ),
        "heads",
    )
    all_channels = channels * lax.axis_size("heads")
    normed_q = (wide_q * lax.rsqrt(sums_q / all_channels + epsilon) * gain_q).astype(jnp.bfloat16)
    normed_k = (wide_k * lax.rsqrt(sums_k / all_channels + epsilon) * gain_k).astype(jnp.bfloat16)
    split_shape = (1, tokens, head_count, head_size)
    space_q = normed_q.reshape(split_shape)
    space_k = normed_k.reshape(split_shape)
    space_v = values.reshape(split_shape)
    time_q, time_k, time_v = (space_q, space_k, space_v)
    slot_heads = jnp.arange(head_count)
    frame_live = frame_valid > 0
    frame_video = (jnp.arange(frame_count) + frame_offset) // video_frames
    own_live = frame_live[position].astype(jnp.float32)
    before = jnp.maximum(position - 1, 0)
    after = jnp.minimum(position + 1, frame_count - 1)
    own_video = frame_video[position]
    ok_before = (position >= 1) & (frame_video[before] == own_video) & frame_live[before]
    ok_after = (position + 1 < frame_count) & (frame_video[after] == own_video) & frame_live[after]
    frame_ok = jnp.stack([ok_before, jnp.array(True), ok_after])
    key_ok = jnp.repeat(frame_ok, tokens)
    kv_pair = jnp.stack([space_k, space_v], axis=1)
    nearby = padded(kv_pair, (("frames", 0),), 1)

    def spatial_slot(slot_index):
        query_all = lax.dynamic_index_in_dim(space_q[0], slot_index, 1, False)
        key_rows = lax.dynamic_index_in_dim(nearby[:, 0], slot_index, 2, False).reshape(
            3 * tokens, head_size
        )
        value_rows = lax.dynamic_index_in_dim(nearby[:, 1], slot_index, 2, False).reshape(
            3 * tokens, head_size
        )
        head_index = slot_heads[slot_index]
        tiles_ok = lax.dynamic_index_in_dim(tile_mask, head_index, 0, False) > 0
        columns_ok = jnp.repeat(tiles_ok, tile_size, axis=1) & key_ok[None, :]

        def one_block(block_index):
            allowed = jnp.repeat(columns_ok, tile_size, axis=0)
            return soft_attend(query_all, key_rows, value_rows, allowed, score_scale)

        result = lax.map(one_block, jnp.arange(tokens // block_rows)).reshape(tokens, head_size)
        return (result * own_live).astype(jnp.bfloat16)

    space_out = lax.map(spatial_slot, jnp.arange(head_count))
    space_out = jnp.transpose(space_out, (1, 0, 2))[None]
    same_video = frame_video[:, None] == frame_video[None, :]
    frame_allowed = frame_live[None, :] & same_video | jnp.eye(frame_count, dtype=bool)
    live_column = frame_live.astype(jnp.float32)[:, None, None, None]
    head_q = lax.all_to_all(time_q, "frames", split_axis=1, concat_axis=0, tiled=True)
    head_k = lax.all_to_all(time_k, "frames", split_axis=1, concat_axis=0, tiled=True)
    head_v = lax.all_to_all(time_v, "frames", split_axis=1, concat_axis=0, tiled=True)
    scores = (
        jnp.einsum("fpnd,gpnd->pnfg", head_q, head_k, preferred_element_type=jnp.float32)
        * score_scale
    )
    scores = jnp.where(frame_allowed, scores, -jnp.inf)
    row_max = jnp.max(scores, axis=3, keepdims=True)
    exp_terms = jnp.exp(scores - row_max)
    row_total = jnp.sum(exp_terms, axis=3, keepdims=True)
    weighted = jnp.einsum(
        "pnfg,gpnd->fpnd",
        exp_terms.astype(jnp.bfloat16),
        head_v,
        preferred_element_type=jnp.float32,
    )
    result = (weighted / jnp.transpose(row_total, (2, 0, 1, 3)) * live_column).astype(jnp.bfloat16)
    time_out = lax.all_to_all(result, "frames", split_axis=0, concat_axis=1, tiled=True)
    spatial_flag = (head_kind == 0)[None, None, :, None]
    attended = jnp.where(spatial_flag, space_out, time_out)
    return attended.reshape(1, tokens, channels)


def solution(mesh):
    placed = (
        P("frames", None, "heads"),
        P("frames", None, "heads"),
        P("frames", None, "heads"),
        P("heads"),
        P("heads"),
        P("heads"),
        P("heads", None, None),
        P(),
    )
    return jax.shard_map(
        local, mesh=mesh, in_specs=placed, out_specs=P("frames", None, "heads"), check_vma=False
    )
```

profile of v0, /device:TPU:1, one launch (start us, length us, event | category | flops | bytes accessed | tf_op | source)
XLA Modules:
  0.0 330.5 jit_solution(9945671259738431445)
XLA Ops:
  0.0 1.4 copy.48
  2.0 18.6 %all-reduce = (f32[1,512,1]{1,2,0:T(1,128)S(1)}, f32[1,512,1]{1,2,0:T(1,128)S(1)}) all-reduce(f32[1,512,1]{1,2,0:T(1,128)S(1)} %bitcast.101, f32[1,512,1]{1,2,0:T(1,128)S(1)} %bitcast.102), channel_id=1, replica_groups=mesh['heads'=8,'frames'=64] {'heads'}, use_global_device_ids=true, to_apply=%region_1.0 | all-reduce | flops 1024 | bytes 8192 | tf_op jit(solution)/shard_map/psum | solution.py:57
  20.9 1.4 copy.54
  22.3 13.2 %all-to-all-start.1 = ((bf16[1,512,5,128]{3,2,0,1:T(8,128)(2,1)}), bf16[1,512,5,128]{3,2,0,1:T(8,128)(2,1)S(1)}, u32[]{:S(2)}, u32[]{:S(2)}) async-start(bf16[1,512,5,128]{3,2,0,1:T(8,128)(2,1)} %copy.54), calls=%async_computation.1 | async-start | bytes 2097152 | tf_op jit(solution)/shard_map/all_to_all | solution.py:111
  35.8 1.4 copy.52
  37.2 47.1 %all-to-all-done.1 = bf16[1,512,5,128]{3,2,0,1:T(8,128)(2,1)S(1)} async-done(((bf16[1,512,5,128]{3,2,0,1:T(8,128)(2,1)}), bf16[1,512,5,128]{3,2,0,1:T(8,128)(2,1)S(1)}, u32[]{:S(2)}, u32[]{:S(2)}) %all-to-all-start.1) | async-done | bytes 655392 | tf_op jit(solution)/shard_map/all_to_all | solution.py:111
  84.3 10.9 %all-to-all-start = ((bf16[1,512,5,128]{3,2,0,1:T(8,128)(2,1)}), bf16[1,512,5,128]{3,2,0,1:T(8,128)(2,1)}, u32[]{:S(2)}, u32[]{:S(2)}) async-start(bf16[1,512,5,128]{3,2,0,1:T(8,128)(2,1)} %copy.52), calls=%async_computation | async-start | bytes 2097152 | tf_op jit(solution)/shard_map/all_to_all | solution.py:110
  96.6 1.5 copy.59
  98.0 45.5 %all-to-all-done = bf16[1,512,5,128]{3,2,0,1:T(8,128)(2,1)} async-done(((bf16[1,512,5,128]{3,2,0,1:T(8,128)(2,1)}), bf16[1,512,5,128]{3,2,0,1:T(8,128)(2,1)}, u32[]{:S(2)}, u32[]{:S(2)}) %all-to-all-start) | async-done | bytes 655392 | tf_op jit(solution)/shard_map/all_to_all | solution.py:110
  143.5 12.1 %all-to-all-start.2 = ((bf16[1,512,5,128]{3,2,0,1:T(8,128)(2,1)}), bf16[1,512,5,128]{3,2,0,1:T(8,128)(2,1)}, u32[]{:S(2)}, u32[]{:S(2)}) async-start(bf16[1,512,5,128]{3,2,0,1:T(8,128)(2,1)} %copy.59), calls=%async_computation.2 | async-start | bytes 2097152 | tf_op jit(solution)/shard_map/all_to_all | solution.py:112
  157.1 5.1 %collective-permute-start = (bf16[1,2,512,5,128]{2,4,3,1,0:T(8,128)(2,1)S(1)}, bf16[1,2,512,5,128]{2,4,3,1,0:T(8,128)(2,1)}, u32[]{:S(2)}, u32[]{:S(2)}) collective-permute-start(bf16[1,2,512,5,128]{2,4,3,1,0:T(8,128)(2,1)S(1)} %pad_maximum_fusion.1), channel_id=1, source_target_pairs={{0,1},{1,2},{2,3},{3,4},{4,5},{5,6},{6,7},{7,8},{8,9},{9,10},{10,1... | collective-permute-start | bytes 3932168 | tf_op jit(solution)/shard_map/ppermute | solution.py:18
  168.1 61.5 %collective-permute-done.1 = bf16[1,2,512,5,128]{2,4,3,1,0:T(8,128)(2,1)} collective-permute-done((bf16[1,2,512,5,128]{2,4,3,1,0:T(8,128)(2,1)S(1)}, bf16[1,2,512,5,128]{2,4,3,1,0:T(8,128)(2,1)}, u32[]{:S(2)}, u32[]{:S(2)}) %collective-permute-start.1) | collective-permute-done | bytes 1310752 | tf_op jit(solution)/shard_map/ppermute | solution.py:19
  229.6 3.5 %pad_maximum_fusion = bf16[3,2,512,5,128]{2,4,3,1,0:T(8,128)(2,1)} fusion(bf16[1,2,512,5,128]{2,4,3,1,0:T(8,128)(2,1)} %collective-permute-done.1, bf16[1,1,512,5,128]{2,4,3,1,0:T(8,128)(2,1)S(1)} %bitcast.94, bf16[1,1,512,5,128]{2,4,3,1,0:T(8,128)(2,1)S(1)} %bitcast.91, bf16[1,2,512,5,128]{2,4,3,1,0:T(8,128)(2,1)} %collective-permute-done), kind=kLoop, calls=%fused_computation.22 | loop fusion | flops 5898240 | bytes 7864320 | tf_op jit(solution)/shard_map/concatenate | solution.py:20
  233.1 6.4 %copy.51 = bf16[3,2,512,5,128]{4,2,0,3,1:T(8,128)(2,1)} copy(bf16[3,2,512,5,128]{2,4,3,1,0:T(8,128)(2,1)} %pad_maximum_fusion) | data formatting | bytes 7864320
  239.4 2.6 fusion.50
  242.4 2.3 fusion.30
  246.0 15.0 %all-to-all-start.3 = ((bf16[64,8,5,128]{3,1,2,0:T(8,128)(2,1)}), bf16[64,8,5,128]{3,1,2,0:T(8,128)(2,1)}, u32[]{:S(2)}, u32[]{:S(2)}) async-start(bf16[64,8,5,128]{3,1,2,0:T(8,128)(2,1)} %copy.63), calls=%async_computation.3 | async-start | bytes 1310720 | tf_op jit(solution)/shard_map/all_to_all | solution.py:128
  261.0 66.7 %while.19 = (s32[]{:T(128)}, bf16[5,512,128]{2,1,0:T(8,128)(2,1)}, s32[5]{0:T(128)S(1)}, s32[5,4,12]{2,1,0:T(4,128)}, bf16[1,512,640]{1,2,0:T(8,128)(2,1)S(1)}, ...) while((s32[]{:T(128)}, bf16[5,512,128]{2,1,0:T(8,128)(2,1)}, ...), condition=%wide.region_7.8_spmd.clone.clone, body=%wide.region_4.7_spmd.clone.clone.sunk | while | flops 408360000 | bytes 21537796 | solution.py:105
  261.0 3.8 %fusion.64 = (bf16[3,1,512,5,128]{4,2,0,3,1:T(8,128)(2,1)S(1)}, bf16[3,1,512,5,128]{4,2,0,3,1:T(8,128)(2,1)}) fusion(bf16[3,2,512,5,128]{4,2,0,3,1:T(8,128)(2,1)} %get-tuple-element.284), kind=kLoop, calls=%fused_computation.60.clone.1 | loop fusion | bytes 7864320 | tf_op jit(solution)/shard_map/while/body/eval_jaxpr/slice | solution.py:88
  274.3 3.8 %fusion.64 = (bf16[3,1,512,5,128]{4,2,0,3,1:T(8,128)(2,1)S(1)}, bf16[3,1,512,5,128]{4,2,0,3,1:T(8,128)(2,1)}) fusion(bf16[3,2,512,5,128]{4,2,0,3,1:T(8,128)(2,1)} %get-tuple-element.284), kind=kLoop, calls=%fused_computation.60.clone.1 | loop fusion | bytes 7864320 | tf_op jit(solution)/shard_map/while/body/eval_jaxpr/slice | solution.py:88
  287.7 3.8 %fusion.64 = (bf16[3,1,512,5,128]{4,2,0,3,1:T(8,128)(2,1)S(1)}, bf16[3,1,512,5,128]{4,2,0,3,1:T(8,128)(2,1)}) fusion(bf16[3,2,512,5,128]{4,2,0,3,1:T(8,128)(2,1)} %get-tuple-element.284), kind=kLoop, calls=%fused_computation.60.clone.1 | loop fusion | bytes 7864320 | tf_op jit(solution)/shard_map/while/body/eval_jaxpr/slice | solution.py:88
  301.0 3.8 %fusion.64 = (bf16[3,1,512,5,128]{4,2,0,3,1:T(8,128)(2,1)S(1)}, bf16[3,1,512,5,128]{4,2,0,3,1:T(8,128)(2,1)}) fusion(bf16[3,2,512,5,128]{4,2,0,3,1:T(8,128)(2,1)} %get-tuple-element.284), kind=kLoop, calls=%fused_computation.60.clone.1 | loop fusion | bytes 7864320 | tf_op jit(solution)/shard_map/while/body/eval_jaxpr/slice | solution.py:88
  314.4 3.8 %fusion.64 = (bf16[3,1,512,5,128]{4,2,0,3,1:T(8,128)(2,1)S(1)}, bf16[3,1,512,5,128]{4,2,0,3,1:T(8,128)(2,1)}) fusion(bf16[3,2,512,5,128]{4,2,0,3,1:T(8,128)(2,1)} %get-tuple-element.284), kind=kLoop, calls=%fused_computation.60.clone.1 | loop fusion | bytes 7864320 | tf_op jit(solution)/shard_map/while/body/eval_jaxpr/slice | solution.py:88
  327.7 1.4 bitcast_select_fusion
  (99 shorter events, 38.3 us)
Async XLA Ops:
  0.0 1.6 copy-start.2
  1.4 19.3 %copy-start.3 = (f32[640]{0:T(1024)S(1)}, f32[640]{0:T(1024)}, u32[]{:S(2)}) copy-start(f32[640]{0:T(1024)} %param.14) | copy-start | bytes 7684
  22.3 13.2 %copy-start.4 = (f32[640]{0:T(1024)S(1)}, f32[640]{0:T(1024)}, u32[]{:S(2)}) copy-start(f32[640]{0:T(1024)} %param.13) | copy-start | bytes 7684
  22.3 61.9 %all-to-all-start.1 = ((bf16[1,512,5,128]{3,2,0,1:T(8,128)(2,1)}), bf16[1,512,5,128]{3,2,0,1:T(8,128)(2,1)S(1)}, u32[]{:S(2)}, u32[]{:S(2)}) async-start(bf16[1,512,5,128]{3,2,0,1:T(8,128)(2,1)} %copy.54), calls=%async_computation.1 | async-start | bytes 2097152 | tf_op jit(solution)/shard_map/all_to_all | solution.py:111
  84.3 12.3 %copy-start = (bf16[1,512,5,128]{3,2,0,1:T(8,128)(2,1)}, bf16[1,512,5,128]{3,2,0,1:T(8,128)(2,1)S(1)}, u32[]{:S(2)}) copy-start(bf16[1,512,5,128]{3,2,0,1:T(8,128)(2,1)S(1)} %all-to-all-done.1) | copy-start | bytes 1966084
  84.3 59.2 %all-to-all-start = ((bf16[1,512,5,128]{3,2,0,1:T(8,128)(2,1)}), bf16[1,512,5,128]{3,2,0,1:T(8,128)(2,1)}, u32[]{:S(2)}, u32[]{:S(2)}) async-start(bf16[1,512,5,128]{3,2,0,1:T(8,128)(2,1)} %copy.52), calls=%async_computation | async-start | bytes 2097152 | tf_op jit(solution)/shard_map/all_to_all | solution.py:110
  143.5 98.9 %all-to-all-start.2 = ((bf16[1,512,5,128]{3,2,0,1:T(8,128)(2,1)}), bf16[1,512,5,128]{3,2,0,1:T(8,128)(2,1)}, u32[]{:S(2)}, u32[]{:S(2)}) async-start(bf16[1,512,5,128]{3,2,0,1:T(8,128)(2,1)} %copy.59), calls=%async_computation.2 | async-start | bytes 2097152 | tf_op jit(solution)/shard_map/all_to_all | solution.py:112
  155.6 6.5 %copy-start.5 = (s32[64]{0:T(128)S(1)}, s32[64]{0:T(128)}, u32[]{:S(2)}) copy-start(s32[64]{0:T(128)} %param.17) | copy-start | bytes 772
  155.7 12.3 %copy-start.6 = (s32[5]{0:T(128)S(1)}, s32[5]{0:T(128)}, u32[]{:S(2)}) copy-start(s32[5]{0:T(128)} %param.15) | copy-start | bytes 64
  155.8 73.8 %collective-permute-start.1 = (bf16[1,2,512,5,128]{2,4,3,1,0:T(8,128)(2,1)S(1)}, bf16[1,2,512,5,128]{2,4,3,1,0:T(8,128)(2,1)}, u32[]{:S(2)}, u32[]{:S(2)}) collective-permute-start(bf16[1,2,512,5,128]{2,4,3,1,0:T(8,128)(2,1)S(1)} %pad_maximum_fusion.1), channel_id=1, source_target_pairs={{1,0},{2,1},{3,2},{4,3},{5,4},{6,5},{7,6},{8,7},{9,8},{10,9},{11,1... | collective-permute-start | bytes 3932168 | tf_op jit(solution)/shard_map/ppermute | solution.py:19
  157.1 72.5 %collective-permute-start = (bf16[1,2,512,5,128]{2,4,3,1,0:T(8,128)(2,1)S(1)}, bf16[1,2,512,5,128]{2,4,3,1,0:T(8,128)(2,1)}, u32[]{:S(2)}, u32[]{:S(2)}) collective-permute-start(bf16[1,2,512,5,128]{2,4,3,1,0:T(8,128)(2,1)S(1)} %pad_maximum_fusion.1), channel_id=1, source_target_pairs={{0,1},{1,2},{2,3},{3,4},{4,5},{5,6},{6,7},{7,8},{8,9},{9,10},{10,1... | collective-permute-start | bytes 3932168 | tf_op jit(solution)/shard_map/ppermute | solution.py:18
  233.1 6.4 %copy-start.1 = (bf16[1,512,5,128]{3,2,0,1:T(8,128)(2,1)S(1)}, bf16[1,512,5,128]{3,2,0,1:T(8,128)(2,1)}, u32[]{:S(2)}) copy-start(bf16[1,512,5,128]{3,2,0,1:T(8,128)(2,1)} %copy-done) | copy-start | bytes 1966084
  246.0 81.7 %all-to-all-start.3 = ((bf16[64,8,5,128]{3,1,2,0:T(8,128)(2,1)}), bf16[64,8,5,128]{3,1,2,0:T(8,128)(2,1)}, u32[]{:S(2)}, u32[]{:S(2)}) async-start(bf16[64,8,5,128]{3,1,2,0:T(8,128)(2,1)} %copy.63), calls=%async_computation.3 | async-start | bytes 1310720 | tf_op jit(solution)/shard_map/all_to_all | solution.py:128
where the time goes:
time: 333 us; the launch traced here: 330 us
  waiting for transfers between devices  154 us (46%)
  starting transfers between devices  57.6 us (17%)
  local copies, waits for them, and re-layouts  49.7 us (15%)
  blocking collectives  18.6 us (6%)
  loops' own time  17.7 us (5%)
  matrix products  15.6 us (5%)
  other arithmetic  12.6 us (4%)
  between operations  4.57 us (1%)
    ppermute x1, waiting for transfers between devices, padded(): after = lax.ppermute(initial, axis, down)  61.5 us
    all_to_all x1, waiting for transfers between devices, local(): lax.all_to_all(time_k, 'frames', split_axis=1, concat_axis=0, tiled=True)  47.1 us
    all_to_all x1, waiting for transfers between devices, local(): lax.all_to_all(time_q, 'frames', split_axis=1, concat_axis=0, tiled=True)  45.5 us
    slice x5, local copies, waits for them, and re-layouts, spatial_slot(): nearby[:, 0]  18.9 us
    psum x1, blocking collectives, local(): lax.psum((jnp.sum(wide_q * wide_q, axis=2, keepdims=True), jnp.sum(wide_k...  18.6 us
    another operation x1, loops' own time, local(): space_out = lax.map(spatial_slot, jnp.arange(head_count))  17.7 us
    all_to_all x1, starting transfers between devices, local(): lax.all_to_all(result, 'frames', split_axis=0, concat_axis=1, tiled=True)  15 us
    all_to_all x1, starting transfers between devices, local(): lax.all_to_all(time_k, 'frames', split_axis=1, concat_axis=0, tiled=True)  13.2 us
  transfers between devices with their start and end apart: 6, of which 3 were waited for; matrix products, arithmetic and copies ran while one was open for 21% of the time, Pallas kernels for 0%

commit v1 on v0

v1 whole, which is shorter than its diff:
```python
import functools
import math

import jax
import jax.numpy as jnp
from jax import lax
from jax.experimental import pallas as pl
from jax.experimental.pallas import tpu as pltpu
from jax.sharding import PartitionSpec as P

epsilon = 1e-06
VIDEO = 32
SHIFT = 8
LOW = -1e30
BF = jnp.bfloat16
F32 = jnp.float32


def params():
    return pltpu.CompilerParams(vmem_limit_bytes=40 * 1024 * 1024)


def head_at(slot, kind_ref, heads):
    flags = [kind_ref[h] for h in range(heads)]
    total = sum(flags)
    found = jnp.int32(0)
    seen = jnp.int32(0)
    for h in range(heads):
        rank = jnp.where(flags[h] > 0, seen, total + h - seen)
        found = jnp.where(rank == slot, h, found)
        seen = seen + flags[h]
    return found


def sums_kernel(groups, tile, q_ref, k_ref, out_ref):
    step = pl.program_id(0)
    steps = pl.num_programs(0)

    def row(ref):
        x = ref[...].astype(F32)
        x = x * x
        part = x[:, :128]
        for g in range(1, groups):
            part = part + x[:, g * 128 : (g + 1) * 128]
        return jnp.sum(part.T, axis=0, keepdims=True)

    copies = out_ref.shape[0]
    out_ref[:, pl.ds(step, 1), :] = jnp.broadcast_to(row(q_ref)[None], (copies, 1, tile))
    out_ref[:, pl.ds(steps + step, 1), :] = jnp.broadcast_to(row(k_ref)[None], (copies, 1, tile))


def local_sums(q, k, copies, tile):
    tokens, channels = q.shape
    steps = tokens // tile
    return pl.pallas_call(
        functools.partial(sums_kernel, channels // 128, tile),
        grid=(steps,),
        in_specs=[pl.BlockSpec((tile, channels), lambda i: (i, 0))] * 2,
        out_specs=pl.BlockSpec((copies, 2 * steps, tile), lambda i: (0, 0, 0)),
        out_shape=jax.ShapeDtypeStruct((copies, 2 * steps, tile), F32),
        compiler_params=params(),
        cost_estimate=pl.CostEstimate(
            flops=4 * q.size, bytes_accessed=4 * q.size, transcendentals=0
        ),
        name="square_sums",
    )(q, k)


def spread_scales(parts_ref, rq, rk, all_channels, tile):
    total = jnp.sum(parts_ref[...], axis=0)
    scale = lax.rsqrt(total / all_channels + epsilon)
    rows = rq.shape[0] // tile
    for c in range(rows):
        here = pl.ds(c * tile, tile)
        rq[here, :] = jnp.broadcast_to(scale[c : c + 1, :], (tile, tile)).T
        rk[here, :] = jnp.broadcast_to(scale[rows + c : rows + c + 1, :], (tile, tile)).T


def pack_kernel(
    all_channels, tile, joined, kind_ref, parts_ref, gq_ref, gk_ref, q_ref, k_ref, v_ref, *rest
):
    rq, rk = rest[-2:]

    @pl.when(pl.program_id(0) == 0)
    def _():
        spread_scales(parts_ref, rq, rk, all_channels, tile)

    normed_q = (q_ref[...].astype(F32) * rq[...] * gq_ref[...]).astype(BF)
    normed_k = (k_ref[...].astype(F32) * rk[...] * gk_ref[...]).astype(BF)
    if joined:
        out_ref = rest[0]
        out_ref[:, 0:128] = normed_q
        out_ref[:, 128:256] = normed_k
        out_ref[:, 256:384] = v_ref[...]
    else:
        kv_ref, qn_ref = rest[:2]
        qn_ref[...] = normed_q
        kv_ref[:, 0:128] = normed_k
        kv_ref[:, 128:256] = v_ref[...]


def pack(kind, parts, gain_q, gain_k, q, k, v, first, count, joined, all_channels, tile):
    tokens, channels = q.shape
    heads = kind.shape[0]
    size = channels // heads

    def column(i, kind_ref):
        return (0, head_at(first + i, kind_ref, heads))

    wide = pl.BlockSpec((tokens, size), column)
    gain = pl.BlockSpec((1, size), column)
    widths = (3,) if joined else (2, 1)
    result = pl.pallas_call(
        functools.partial(pack_kernel, all_channels, tile, joined),
        grid_spec=pltpu.PrefetchScalarGridSpec(
            num_scalar_prefetch=1,
            grid=(count,),
            in_specs=[
                pl.BlockSpec(parts.shape, lambda i, kind_ref: (0, 0, 0)),
                gain,
                gain,
                wide,
                wide,
                wide,
            ],
            out_specs=[
                pl.BlockSpec((tokens, w * size), lambda i, kind_ref: (0, i)) for w in widths
            ],
            scratch_shapes=[pltpu.VMEM((tokens, size), F32)] * 2,
        ),
        out_shape=[jax.ShapeDtypeStruct((tokens, w * size * count), BF) for w in widths],
        compiler_params=params(),
        cost_estimate=pl.CostEstimate(
            flops=4 * tokens * size * count,
            bytes_accessed=12 * tokens * size * count,
            transcendentals=0,
        ),
        name="pack_temporal" if joined else "pack_spatial",
    )(kind, parts, gain_q, gain_k, q, k, v)
    return result


def temporal_kernel(scale, tokens, x_ref, live_ref, out_ref, bias):
    rows = x_ref.shape[0]

    @pl.when(pl.program_id(0) == 0)
    def _():
        at_row = lax.broadcasted_iota(jnp.int32, (rows, rows), 0)
        at_col = lax.broadcasted_iota(jnp.int32, (rows, rows), 1)
        bits = tokens.bit_length() - 1
        frame_row, frame_col = at_row >> bits, at_col >> bits
        same_token = (at_row & (tokens - 1)) == (at_col & (tokens - 1))
        video_bits = VIDEO.bit_length() - 1
        same_video = ((frame_row + SHIFT) >> video_bits) == ((frame_col + SHIFT) >> video_bits)
        live = live_ref[...] > 0
        allowed = same_token & ((frame_row == frame_col) | (same_video & live))
        bias[...] = jnp.where(allowed, 0.0, LOW).astype(F32)

    s = lax.dot_general(
        x_ref[:, 0:128], x_ref[:, 128:256], (((1,), (1,)), ((), ())), preferred_element_type=F32
    )
    s = s * scale + bias[...]
    p = jnp.exp(s - jnp.max(s, axis=1, keepdims=True))
    total = jnp.sum(p, axis=1, keepdims=True)
    o = jnp.dot(p.astype(BF), x_ref[:, 256:384], preferred_element_type=F32)
    out_ref[...] = (o / total).astype(BF)


def temporal(x, live_row, count, tokens, size, scale):
    rows = x.shape[0]
    return pl.pallas_call(
        functools.partial(temporal_kernel, scale, tokens),
        grid=(count,),
        in_specs=[
            pl.BlockSpec((rows, 3 * size), lambda i: (0, i)),
            pl.BlockSpec((1, rows), lambda i: (0, 0)),
        ],
        out_specs=pl.BlockSpec((rows, size), lambda i: (0, i)),
        out_shape=jax.ShapeDtypeStruct((rows, count * size), BF),
        scratch_shapes=[pltpu.VMEM((rows, rows), F32)],
        compiler_params=params(),
        cost_estimate=pl.CostEstimate(
            flops=4 * rows * rows * size * count,
            bytes_accessed=8 * rows * size * count,
            transcendentals=rows * rows * count,
        ),
        name="temporal_heads",
    )(x, live_row)


def spatial_kernel(
    scale, tile, first, kind_ref, mask_ref, near_ref, q_ref, own_ref, before_ref, after_ref, out_ref
):
    heads = kind_ref.shape[0]
    head = head_at(first + pl.program_id(0), kind_ref, heads)
    tokens = q_ref.shape[0]
    tiles = tokens // tile
    frames = (before_ref, own_ref, after_ref)
    own_live = near_ref[3].astype(F32)
    for i in range(tiles):
        rows = pl.ds(i * tile, tile)
        q = q_ref[rows, :]
        pieces = []
        for o in range(3):
            s = lax.dot_general(
                q, frames[o][:, 0:128], (((1,), (1,)), ((), ())), preferred_element_type=F32
            )
            for j in range(tiles):
                ok = (mask_ref[head, i, o * tiles + j] > 0) & (near_ref[o] > 0)
                low = jnp.where(ok, 0.0, LOW).astype(F32)
                pieces.append(s[:, j * tile : (j + 1) * tile] * scale + low)
        top = pieces[0]
        for x in pieces[1:]:
            top = jnp.maximum(top, x)
        top = jnp.max(top, axis=1, keepdims=True)
        pieces = [jnp.exp(x - top) for x in pieces]
        total = pieces[0]
        for x in pieces[1:]:
            total = total + x
        total = jnp.sum(total, axis=1, keepdims=True)
        o_sum = None
        for o in range(3):
            p = jnp.concatenate([x.astype(BF) for x in pieces[o * tiles : (o + 1) * tiles]], axis=1)
            part = jnp.dot(p, frames[o][:, 128:256], preferred_element_type=F32)
            o_sum = part if o_sum is None else o_sum + part
        out_ref[rows, :] = (o_sum / total * own_live).astype(BF)


def spatial(kind, mask, near, q, own, before, after, first, count, channels, scale, tile):
    tokens = q.shape[0]
    heads = kind.shape[0]
    size = channels // heads

    def slot(i, *_):
        return (0, i)

    return pl.pallas_call(
        functools.partial(spatial_kernel, scale, tile, first),
        grid_spec=pltpu.PrefetchScalarGridSpec(
            num_scalar_prefetch=3,
            grid=(count,),
            in_specs=[pl.BlockSpec((tokens, size), slot)]
            + [pl.BlockSpec((tokens, 2 * size), slot)] * 3,
            out_specs=pl.BlockSpec(
                (tokens, size),
                lambda i, kind_ref, *_: (0, head_at(first + i, kind_ref, heads)),
            ),
        ),
        out_shape=jax.ShapeDtypeStruct((tokens, channels), BF),
        compiler_params=params(),
        cost_estimate=pl.CostEstimate(
            flops=12 * tokens * tokens * size * count,
            bytes_accessed=16 * tokens * size * count,
            transcendentals=3 * tokens * tokens * count,
        ),
        name="spatial_heads",
    )(kind, mask, near, q, own, before, after)


def merge_kernel(kind_ref, near_ref, base_ref, x_ref, out_ref):
    x = x_ref[...]
    out_ref[...] = jnp.where(near_ref[3] > 0, x, jnp.zeros_like(x))


def merge(kind, near, base, x, count):
    tokens, channels = base.shape
    heads = kind.shape[0]
    size = channels // heads
    return pl.pallas_call(
        merge_kernel,
        grid_spec=pltpu.PrefetchScalarGridSpec(
            num_scalar_prefetch=2,
            grid=(count,),
            in_specs=[
                pl.BlockSpec(memory_space=pl.ANY),
                pl.BlockSpec((tokens, size), lambda i, *_: (0, i)),
            ],
            out_specs=pl.BlockSpec(
                (tokens, size), lambda i, kind_ref, *_: (0, head_at(i, kind_ref, heads))
            ),
        ),
        out_shape=jax.ShapeDtypeStruct((tokens, channels), BF),
        input_output_aliases={2: 0},
        compiler_params=params(),
        cost_estimate=pl.CostEstimate(
            flops=0, bytes_accessed=4 * tokens * size * count, transcendentals=0
        ),
        name="merge_heads",
    )(kind, near, base, x)


def local(queries, keys, values, gain_q, gain_k, head_kind, tile_mask, frame_valid):
    heads = head_kind.shape[0]
    tokens, channels = queries.shape[1:]
    size = channels // heads
    tile = tokens // tile_mask.shape[1]
    frames = lax.axis_size("frames")
    blocks = lax.axis_size("heads")
    position = lax.axis_index("frames")
    scale = 1.0 / math.sqrt(size)
    share = tokens // frames
    q, k, v = queries[0], keys[0], values[0]

    parts = local_sums(q, k, blocks, tile)
    parts = lax.all_to_all(parts, "heads", split_axis=0, concat_axis=0, tiled=True)

    live = (frame_valid > 0).astype(jnp.int32)
    video = (jnp.arange(frames) + SHIFT) // VIDEO
    before = jnp.maximum(position - 1, 0)
    after = jnp.minimum(position + 1, frames - 1)
    ok_before = (position >= 1) & (video[before] == video[position]) & (live[before] > 0)
    ok_after = (position + 1 < frames) & (video[after] == video[position]) & (live[after] > 0)
    near = jnp.stack(
        [ok_before.astype(jnp.int32), jnp.int32(1), ok_after.astype(jnp.int32), live[position]]
    )
    live_row = jnp.repeat(live, share)[None, :].astype(F32)
    rows_q, rows_k = gain_q[None, :], gain_k[None, :]
    up = [(i, i + 1) for i in range(frames - 1)]
    down = [(j, i) for i, j in up]

    def exchange(x):
        x = x.reshape(frames, share, x.shape[1])
        return lax.all_to_all(x, "frames", split_axis=0, concat_axis=0, tiled=True).reshape(
            tokens, x.shape[2]
        )

    def branch(count):
        rest = heads - count

        def run(q, k, v, parts):
            args = (head_kind, parts, rows_q, rows_k, q, k, v)
            (sent,) = pack(*args, 0, count, True, blocks * channels, tile)
            mine = exchange(sent)
            pair, near_q = pack(*args, count, rest, False, blocks * channels, tile)
            earlier = lax.ppermute(pair, "frames", up)
            later = lax.ppermute(pair, "frames", down)
            told = temporal(mine, live_row, count, share, size, scale)
            back = exchange(told)
            base = spatial(
                head_kind, tile_mask, near, near_q, pair, earlier, later,
                count, rest, channels, scale, tile,
            )
            return merge(head_kind, near, base, back, count)

        return run

    choice = jnp.sum(head_kind) - 1
    out = lax.switch(choice, [branch(c) for c in range(1, heads)], q, k, v, parts)
    return out[None]


def solution(mesh):
    placed = (
        P("frames", None, "heads"),
        P("frames", None, "heads"),
        P("frames", None, "heads"),
        P("heads"),
        P("heads"),
        P("heads"),
        P("heads", None, None),
        P(),
    )
    return jax.shard_map(
        local, mesh=mesh, in_specs=placed, out_specs=P("frames", None, "heads"), check_vma=False
    )
```

time: 333 us -> 165 us (0.50)
  waiting for transfers between devices: 154 us -> 94.8 us
  local copies, waits for them, and re-layouts: 49.7 us -> 3.08 us
  blocking collectives: 18.6 us -> 0 us
  Pallas kernels: 0 us -> 17.5 us
  starting transfers between devices: 57.6 us -> 40.1 us
  loops' own time: 17.7 us -> 0.34 us
  matrix products: 15.6 us -> 0 us
  other arithmetic: 12.6 us -> 2.59 us
    ppermute x2, waiting for transfers between devices: 61.5 us -> 23.2 us  [the longest x1 21.1 us: run(): earlier = lax.ppermute(pair, 'frames', up)]
    all_to_all x4 -> x3, waiting for transfers between devices: 92.5 us -> 71.5 us  [the longest x2 71.5 us: exchange(): lax.all_to_all(x, 'frames', split_axis=0, concat_axis=0, tiled=True)]
    slice x5 -> x0, local copies, waits for them, and re-layouts: 18.9 us -> none  [spatial_slot(): nearby[:, 0]]
    psum x1 -> x0, blocking collectives: 18.6 us -> none  [local(): lax.psum((jnp.sum(wide_q * wide_q, axis=2, keepdims=True), jnp.sum(wide_k...]
    pallas_call x0 -> x6, Pallas kernels: none -> 17.5 us  [the longest x2 6.32 us: pack(): pl.pallas_call(functools.partial(pack_kernel, all_channels, tile, joined)...]
    another operation x1, loops' own time: 17.7 us -> 0.34 us  [local(): lax.switch(choice, [branch(c) for c in range(1, heads)], q, k, v, parts)]
    dot_general x12 -> x0, matrix products: 15.6 us -> none  [the longest x5 6.52 us: soft_attend(): jnp.dot(exp_terms.astype(jnp.bfloat16), value_rows, preferred_element_typ...]
    all_to_all x4 -> x3, starting transfers between devices: 51.2 us -> 35.9 us  [the longest x2 25.8 us: exchange(): lax.all_to_all(x, 'frames', split_axis=0, concat_axis=0, tiled=True)]
  transfers between devices with their start and end apart: 6 -> 5, of which waited for: 3 -> 3; matrix products, arithmetic and copies ran while one was open for 21% -> 2% of each run, Pallas kernels for 0% -> 3%
where the time goes in v1:
time: 165 us; the launch traced here: 163 us
  waiting for transfers between devices  94.8 us (57%)
  starting transfers between devices  40.1 us (24%)
  Pallas kernels  17.5 us (11%)
  between operations  4.36 us (3%)
  local copies, waits for them, and re-layouts  3.08 us (2%)
  other arithmetic  2.59 us (2%)
    all_to_all x2, waiting for transfers between devices, exchange(): lax.all_to_all(x, 'frames', split_axis=0, concat_axis=0, tiled=True)  71.5 us
    all_to_all x2, starting transfers between devices, exchange(): lax.all_to_all(x, 'frames', split_axis=0, concat_axis=0, tiled=True)  25.8 us
    ppermute x1, waiting for transfers between devices, run(): earlier = lax.ppermute(pair, 'frames', up)  21.1 us
    all_to_all x1, starting transfers between devices, local(): lax.all_to_all(parts, 'heads', split_axis=0, concat_axis=0, tiled=True)  10.1 us
    pallas_call x2, Pallas kernels, pack(): pl.pallas_call(functools.partial(pack_kernel, all_channels, tile, joined)...  6.32 us
    pallas_call x1, Pallas kernels, temporal(): pl.pallas_call(functools.partial(temporal_kernel, scale, tokens), grid=(c...  4.38 us
  transfers between devices with their start and end apart: 5, of which 3 were waited for; matrix products, arithmetic and copies ran while one was open for 2% of the time, Pallas kernels for 3%

profile of v1, /device:TPU:1, one launch (start us, length us, event | category | flops | bytes accessed | tf_op | source)
XLA Modules:
  0.0 162.7 jit_solution(11030486151342361283)
XLA Ops:
  0.0 3.1 %square_sums.1 = f32[8,8,128]{2,1,0:T(8,128)} custom-call(bf16[512,640]{1,0:T(8,128)(2,1)} %bitcast.40, bf16[512,640]{1,0:T(8,128)(2,1)} %bitcast.45), custom_call_target="tpu_custom_call" | custom-call | flops 1310720 | bytes 1310720 | tf_op jit(solution)/shard_map/square_sums/pallas_call | solution.py:55
  3.1 10.1 %all-to-all-start.8 = ((f32[8,8,128]{2,1,0:T(8,128)}), f32[8,8,128]{2,1,0:T(8,128)S(1)}, u32[]{:S(2)}, u32[]{:S(2)}) async-start(f32[8,8,128]{2,1,0:T(8,128)} %square_sums.1), calls=%async_computation.8 | async-start | bytes 65536 | tf_op jit(solution)/shard_map/all_to_all | solution.py:305
  13.2 0.7 fusion
  13.9 0.7 fusion.1
  18.3 0.6 pad_add_fusion
  19.0 1.3 reduce_sum.9
  20.8 141.9 %conditional.1 = (bf16[1,512,640]{2,1,0:T(8,128)(2,1)}) conditional(s32[]{:T(128)} %clamp.3, (s32[5]{0:T(128)}, f32[8,8,128]{2,1,0:T(8,128)S(1)}, f32[640]{0:T(1024)}, f32[640]{0:T(1024)}, bf16[512,640]{1,0:T(8,128)(2,1)}, /*index=5*/bf16[512,640]{1,0:T(8,128)(2,1)}, bf16[1,512,640]{2,1,0:T(8,128)(2,1)}, ...), branch_computations={%region_1.2_spmd, %region_2.3_spmd, %region_3.4_spmd, %region_4.5_... | conditional | flops 1746141184 | bytes 30950032 | solution.py:348
  21.1 0.7 broadcast_in_dim.28.gq_ref
  21.8 0.7 broadcast_in_dim.32.gk_ref
  22.4 4.8 %pack_temporal.7 = bf16[512,1536]{1,0:T(8,128)(2,1)} custom-call(s32[5]{0:T(128)} %get-tuple-element.127.kind_ref, f32[8,8,128]{2,1,0:T(8,128)S(1)} %get-tuple-element.130.parts_ref, f32[1,640]{1,0:T(1,128)S(1)} %broadcast_in_dim.28.gq_ref, f32[1,640]{1,0:T(1,128)S(1)} %broadcast_in_dim.32.gk_ref, bf16[512,640]{1,0:T(8,128)(2,1)} %get-tuple-element.133.q_ref, ...), custom_call_target="tpu_custom_call" | custom-call | flops 1048576 | bytes 3145728 | tf_op jit(solution)/shard_map/cond/branch_3_fun/pack_temporal/pallas_call | solution.py:113
  27.2 14.1 %all-to-all-start.6 = ((bf16[64,8,1536]{2,1,0:T(8,128)(2,1)}), bf16[64,8,1536]{2,1,0:T(8,128)(2,1)S(1)}, u32[]{:S(2)}, u32[]{:S(2)}) async-start(bf16[64,8,1536]{2,1,0:T(8,128)(2,1)} %bitcast.19), calls=%async_computation.6 | async-start | bytes 3145728 | tf_op jit(solution)/shard_map/cond/branch_3_fun/all_to_all | solution.py:323
  41.4 0.1 broadcast_in_dim.36
  41.4 0.1 convert_element_type.26.live_ref
  41.5 71.5 %all-to-all-done.6 = bf16[64,8,1536]{2,1,0:T(8,128)(2,1)S(1)} async-done(((bf16[64,8,1536]{2,1,0:T(8,128)(2,1)}), bf16[64,8,1536]{2,1,0:T(8,128)(2,1)S(1)}, u32[]{:S(2)}, u32[]{:S(2)}) %all-to-all-start.6) | async-done | bytes 1572896 | tf_op jit(solution)/shard_map/cond/branch_3_fun/all_to_all | solution.py:323
  113.1 4.4 %temporal_heads.7 = bf16[512,512]{1,0:T(8,128)(2,1)} custom-call(bf16[512,1536]{1,0:T(8,128)(2,1)S(1)} %bitcast.32, f32[1,512]{1,0:T(1,128)S(1)} %convert_element_type.26.live_ref), custom_call_target="tpu_custom_call" | custom-call | flops 536870912 | bytes 2097152 | tf_op jit(solution)/shard_map/cond/branch_3_fun/temporal_heads/pallas_call | solution.py:171
  117.5 11.6 %all-to-all-start.7 = ((bf16[64,8,512]{2,1,0:T(8,128)(2,1)}), bf16[64,8,512]{2,1,0:T(8,128)(2,1)S(1)}, u32[]{:S(2)}, u32[]{:S(2)}) async-start(bf16[64,8,512]{2,1,0:T(8,128)(2,1)} %bitcast.21), calls=%async_computation.7 | async-start | bytes 1048576 | tf_op jit(solution)/shard_map/cond/branch_3_fun/all_to_all | solution.py:323
  129.2 1.5 pack_spatial.7
  130.7 2.9 %collective-permute-start.6 = (bf16[512,256]{1,0:T(8,128)(2,1)S(1)}, bf16[512,256]{1,0:T(8,128)(2,1)S(1)}, u32[]{:S(2)}, u32[]{:S(2)}) collective-permute-start(bf16[512,256]{1,0:T(8,128)(2,1)S(1)} %get-tuple-element.137.own_ref), channel_id=1, source_target_pairs={{0,1},{1,2},{2,3},{3,4},{4,5},{5,6},{6,7},{7,8},{8,9},{9,10},{10,1... | collective-permute-start | bytes 786440 | tf_op jit(solution)/shard_map/cond/branch_3_fun/ppermute | solution.py:335
  133.7 1.3 collective-permute-start.7
  135.0 21.1 %collective-permute-done.6.before_ref = bf16[512,256]{1,0:T(8,128)(2,1)S(1)} collective-permute-done((bf16[512,256]{1,0:T(8,128)(2,1)S(1)}, bf16[512,256]{1,0:T(8,128)(2,1)S(1)}, u32[]{:S(2)}, u32[]{:S(2)}) %collective-permute-start.6) | collective-permute-done | bytes 262176 | tf_op jit(solution)/shard_map/cond/branch_3_fun/ppermute | solution.py:335
  156.0 2.2 %collective-permute-done.7.after_ref = bf16[512,256]{1,0:T(8,128)(2,1)S(1)} collective-permute-done((bf16[512,256]{1,0:T(8,128)(2,1)S(1)}, bf16[512,256]{1,0:T(8,128)(2,1)S(1)}, u32[]{:S(2)}, u32[]{:S(2)}) %collective-permute-start.7) | collective-permute-done | bytes 262176 | tf_op jit(solution)/shard_map/cond/branch_3_fun/ppermute | solution.py:336
  158.2 2.6 %spatial_heads.7.base_ref = bf16[512,640]{1,0:T(8,128)(2,1)S(1)} custom-call(s32[5]{0:T(128)S(1)} %copy-done.22, s32[5,4,12]{2,1,0:T(4,128)S(1)} %copy-done.27, s32[4]{0:T(128)S(1)} %copy-done.24, bf16[512,128]{1,0:T(8,128)(2,1)S(1)} %get-tuple-element.136.q_ref, bf16[512,256]{1,0:T(8,128)(2,1)S(1)} %get-tuple-element.137.own_ref, ...), custom_call_target="tpu_custom_call" | custom-call | flops 402653184 | bytes 1048576 | tf_op jit(solution)/shard_map/cond/branch_3_fun/spatial_heads/pallas_call | solution.py:237
  160.8 1.1 merge_heads.7
  161.9 0.8 copy-done.16
  (20 shorter events, 0.0 us)
Async XLA Ops:
  3.1 17.7 %all-to-all-start.8 = ((f32[8,8,128]{2,1,0:T(8,128)}), f32[8,8,128]{2,1,0:T(8,128)S(1)}, u32[]{:S(2)}, u32[]{:S(2)}) async-start(f32[8,8,128]{2,1,0:T(8,128)} %square_sums.1), calls=%async_computation.8 | async-start | bytes 65536 | tf_op jit(solution)/shard_map/all_to_all | solution.py:305
  21.0 6.2 %copy-start.18 = (f32[8,8,128]{2,1,0:T(8,128)}, f32[8,8,128]{2,1,0:T(8,128)S(1)}, u32[]{:S(2)}) copy-start(f32[8,8,128]{2,1,0:T(8,128)S(1)} %get-tuple-element.130.parts_ref) | copy-start | bytes 98308 | tf_op jit(solution)/shard_map/cond
  21.0 6.2 %copy-start.23 = (s32[4]{0:T(128)}, s32[4]{0:T(128)S(1)}, u32[]{:S(2)}) copy-start(s32[4]{0:T(128)S(1)} %get-tuple-element.128.near_ref) | copy-start | bytes 52 | tf_op jit(solution)/shard_map/cond
  27.2 85.9 %all-to-all-start.6 = ((bf16[64,8,1536]{2,1,0:T(8,128)(2,1)}), bf16[64,8,1536]{2,1,0:T(8,128)(2,1)S(1)}, u32[]{:S(2)}, u32[]{:S(2)}) async-start(bf16[64,8,1536]{2,1,0:T(8,128)(2,1)} %bitcast.19), calls=%async_computation.6 | async-start | bytes 3145728 | tf_op jit(solution)/shard_map/cond/branch_3_fun/all_to_all | solution.py:323
  113.1 16.0 %copy-start.5 = (bf16[512,640]{1,0:T(8,128)(2,1)S(1)}, bf16[512,640]{1,0:T(8,128)(2,1)}, u32[]{:S(2)}) copy-start(bf16[512,640]{1,0:T(8,128)(2,1)} %get-tuple-element.133.q_ref) | copy-start | bytes 1966084 | tf_op jit(solution)/shard_map/cond
  113.1 16.1 %copy-start.9 = (bf16[512,640]{1,0:T(8,128)(2,1)S(1)}, bf16[512,640]{1,0:T(8,128)(2,1)}, u32[]{:S(2)}) copy-start(bf16[512,640]{1,0:T(8,128)(2,1)} %get-tuple-element.134.k_ref) | copy-start | bytes 1966084 | tf_op jit(solution)/shard_map/cond
  113.1 16.1 %copy-start.13 = (bf16[1,512,640]{2,1,0:T(8,128)(2,1)S(1)}, bf16[1,512,640]{2,1,0:T(8,128)(2,1)}, u32[]{:S(2)}) copy-start(bf16[1,512,640]{2,1,0:T(8,128)(2,1)} %get-tuple-element.191) | copy-start | bytes 1966084 | tf_op jit(solution)/shard_map/cond
  113.1 16.1 %copy-start.22 = (s32[5]{0:T(128)S(1)}, s32[5]{0:T(128)}, u32[]{:S(2)}) copy-start(s32[5]{0:T(128)} %get-tuple-element.127.kind_ref) | copy-start | bytes 64 | tf_op jit(solution)/shard_map/cond
  117.5 40.7 %copy-start.24 = (s32[4]{0:T(128)S(1)}, s32[4]{0:T(128)}, u32[]{:S(2)}) copy-start(s32[4]{0:T(128)} %copy-done.23) | copy-start | bytes 52 | tf_op jit(solution)/shard_map/cond
  117.5 40.7 %copy-start.27 = (s32[5,4,12]{2,1,0:T(4,128)S(1)}, s32[5,4,12]{2,1,0:T(4,128)}, u32[]{:S(2)}) copy-start(s32[5,4,12]{2,1,0:T(4,128)} %get-tuple-element.175.mask_ref) | copy-start | bytes 2884 | tf_op jit(solution)/shard_map/cond
  117.5 43.3 %all-to-all-start.7 = ((bf16[64,8,512]{2,1,0:T(8,128)(2,1)}), bf16[64,8,512]{2,1,0:T(8,128)(2,1)S(1)}, u32[]{:S(2)}, u32[]{:S(2)}) async-start(bf16[64,8,512]{2,1,0:T(8,128)(2,1)} %bitcast.21), calls=%async_computation.7 | async-start | bytes 1048576 | tf_op jit(solution)/shard_map/cond/branch_3_fun/all_to_all | solution.py:323
  130.7 25.3 %collective-permute-start.6 = (bf16[512,256]{1,0:T(8,128)(2,1)S(1)}, bf16[512,256]{1,0:T(8,128)(2,1)S(1)}, u32[]{:S(2)}, u32[]{:S(2)}) collective-permute-start(bf16[512,256]{1,0:T(8,128)(2,1)S(1)} %get-tuple-element.137.own_ref), channel_id=1, source_target_pairs={{0,1},{1,2},{2,3},{3,4},{4,5},{5,6},{6,7},{7,8},{8,9},{9,10},{10,1... | collective-permute-start | bytes 786440 | tf_op jit(solution)/shard_map/cond/branch_3_fun/ppermute | solution.py:335
  133.7 24.5 %collective-permute-start.7 = (bf16[512,256]{1,0:T(8,128)(2,1)S(1)}, bf16[512,256]{1,0:T(8,128)(2,1)S(1)}, u32[]{:S(2)}, u32[]{:S(2)}) collective-permute-start(bf16[512,256]{1,0:T(8,128)(2,1)S(1)} %get-tuple-element.137.own_ref), channel_id=1, source_target_pairs={{1,0},{2,1},{3,2},{4,3},{5,4},{6,5},{7,6},{8,7},{9,8},{10,9},{11,1... | collective-permute-start | bytes 786440 | tf_op jit(solution)/shard_map/cond/branch_3_fun/ppermute | solution.py:336
  161.9 0.8 copy-start.16

commit v2 on v1

v2 whole, which is shorter than its diff:
```python
import functools
import math

import jax
import jax.numpy as jnp
from jax import lax
from jax.experimental import pallas as pl
from jax.experimental.pallas import tpu as pltpu
from jax.sharding import PartitionSpec as P

epsilon = 1e-06
VIDEO = 32
SHIFT = 8
LOW = -1e30
BF = jnp.bfloat16
F32 = jnp.float32


def params():
    return pltpu.CompilerParams(vmem_limit_bytes=40 * 1024 * 1024)


def head_at(slot, kind_ref, heads):
    flags = [kind_ref[h] for h in range(heads)]
    total = sum(flags)
    found = jnp.int32(0)
    seen = jnp.int32(0)
    for h in range(heads):
        rank = jnp.where(flags[h] > 0, seen, total + h - seen)
        found = jnp.where(rank == slot, h, found)
        seen = seen + flags[h]
    return found


def sums_kernel(groups, tile, q_ref, k_ref, out_ref, q_buf, k_buf, sems):
    tokens = q_ref.shape[0]
    steps = tokens // tile
    copies = []
    for i in range(steps):
        rows = pl.ds(i * tile, tile)
        for n, (ref, buf) in enumerate(((q_ref, q_buf), (k_ref, k_buf))):
            copy = pltpu.make_async_copy(ref.at[rows, :], buf.at[rows, :], sems.at[2 * i + n])
            copy.start()
            copies.append(copy)
    for i in range(steps):
        for n, buf in enumerate((q_buf, k_buf)):
            copies[2 * i + n].wait()
            x = buf[pl.ds(i * tile, tile), :].astype(F32)
            x = x * x
            part = x[:, :128]
            for g in range(1, groups):
                part = part + x[:, g * 128 : (g + 1) * 128]
            row = jnp.sum(part.T, axis=0, keepdims=True)
            at = n * steps + i
            out_ref[:, at : at + 1, :] = jnp.broadcast_to(row[None], (out_ref.shape[0], 1, tile))


def local_sums(q, k, copies, tile):
    tokens, channels = q.shape
    steps = tokens // tile
    return pl.pallas_call(
        functools.partial(sums_kernel, channels // 128, tile),
        in_specs=[pl.BlockSpec(memory_space=pl.ANY)] * 2,
        out_specs=pl.BlockSpec(memory_space=pltpu.VMEM),
        out_shape=jax.ShapeDtypeStruct((copies, 2 * steps, tile), F32),
        scratch_shapes=[pltpu.VMEM((tokens, channels), BF)] * 2
        + [pltpu.SemaphoreType.DMA((2 * steps,))],
        compiler_params=params(),
        cost_estimate=pl.CostEstimate(
            flops=4 * q.size, bytes_accessed=4 * q.size, transcendentals=0
        ),
        name="square_sums",
    )(q, k)


def pack_kernel(
    all_channels, tile, first, count, joined,
    kind_ref, parts_ref, gq_ref, gk_ref, q_ref, k_ref, v_ref, *rest
):
    if joined:
        out_ref, q_buf, k_buf, out_buf, rq, rk, in_sems, out_sems = rest
    else:
        out_ref, qn_ref, q_buf, k_buf, out_buf, rq, rk, in_sems, out_sems = rest
    tokens = q_ref.shape[0]
    heads = kind_ref.shape[0]
    size = q_ref.shape[1] // heads
    width = out_buf.shape[2]
    starts = []
    copies = []
    for s in range(count):
        start = pl.multiple_of(head_at(first + s, kind_ref, heads) * size, size)
        starts.append(start)
        columns = pl.ds(start, size)
        trio = (
            (q_ref, q_buf.at[s]),
            (k_ref, k_buf.at[s]),
            (v_ref, out_buf.at[s, :, pl.ds(width - size, size)]),
        )
        for n, (ref, buf) in enumerate(trio):
            copy = pltpu.make_async_copy(ref.at[:, columns], buf, in_sems.at[3 * s + n])
            copy.start()
            copies.append(copy)
    total = jnp.sum(parts_ref[...], axis=0)
    scale = lax.rsqrt(total / all_channels + epsilon)
    rows = tokens // tile
    for c in range(rows):
        here = pl.ds(c * tile, tile)
        rq[here, :] = jnp.broadcast_to(scale[c : c + 1, :], (tile, tile)).T
        rk[here, :] = jnp.broadcast_to(scale[rows + c : rows + c + 1, :], (tile, tile)).T
    outs = []
    for s in range(count):
        gain_q = gq_ref[pl.ds(starts[s], size)].reshape(1, size)
        gain_k = gk_ref[pl.ds(starts[s], size)].reshape(1, size)
        copies[3 * s].wait()
        normed_q = (q_buf[s].astype(F32) * rq[...] * gain_q).astype(BF)
        copies[3 * s + 1].wait()
        normed_k = (k_buf[s].astype(F32) * rk[...] * gain_k).astype(BF)
        if joined:
            out_buf[s, :, 0:size] = normed_q
            out_buf[s, :, size : 2 * size] = normed_k
        else:
            qn_ref[:, s * size : (s + 1) * size] = normed_q
            out_buf[s, :, 0:size] = normed_k
        copies[3 * s + 2].wait()
        out = pltpu.make_async_copy(
            out_buf.at[s], out_ref.at[:, pl.ds(s * width, width)], out_sems.at[s]
        )
        out.start()
        outs.append(out)
    for out in outs:
        out.wait()


def pack(kind, parts, gain_q, gain_k, q, k, v, first, count, joined, all_channels, tile):
    tokens, channels = q.shape
    size = channels // kind.shape[0]
    width = (3 if joined else 2) * size
    out_shape = [jax.ShapeDtypeStruct((tokens, count * width), BF)]
    out_specs = [pl.BlockSpec(memory_space=pl.ANY)]
    if not joined:
        out_shape.append(jax.ShapeDtypeStruct((tokens, count * size), BF))
        out_specs.append(pl.BlockSpec(memory_space=pltpu.VMEM))
    return pl.pallas_call(
        functools.partial(pack_kernel, all_channels, tile, first, count, joined),
        in_specs=[pl.BlockSpec(memory_space=pltpu.SMEM)]
        + [pl.BlockSpec(memory_space=pltpu.VMEM)] * 3
        + [pl.BlockSpec(memory_space=pl.ANY)] * 3,
        out_specs=out_specs,
        out_shape=out_shape,
        scratch_shapes=[
            pltpu.VMEM((count, tokens, size), BF),
            pltpu.VMEM((count, tokens, size), BF),
            pltpu.VMEM((count, tokens, width), BF),
            pltpu.VMEM((tokens, size), F32),
            pltpu.VMEM((tokens, size), F32),
            pltpu.SemaphoreType.DMA((3 * count,)),
            pltpu.SemaphoreType.DMA((count,)),
        ],
        compiler_params=params(),
        cost_estimate=pl.CostEstimate(
            flops=4 * tokens * size * count,
            bytes_accessed=12 * tokens * size * count,
            transcendentals=0,
        ),
        name="pack_temporal" if joined else "pack_spatial",
    )(kind, parts, gain_q, gain_k, q, k, v)


def video_rows(frames, share):
    spans = []
    start = 0
    while start < frames:
        stop = min(frames, ((start + SHIFT) // VIDEO + 1) * VIDEO - SHIFT)
        spans.append((start * share, stop * share))
        start = stop
    return spans


def temporal_kernel(scale, count, share, x_ref, valid_ref, *rest):
    out_ref, x_buf, out_buf, live_buf, in_sems, out_sems = rest[-6:]
    rows = x_ref.shape[0]
    frames = valid_ref.shape[1]
    size = out_buf.shape[2]
    copies = []
    for s in range(count):
        copy = pltpu.make_async_copy(
            x_ref.at[:, pl.ds(s * 3 * size, 3 * size)], x_buf.at[s], in_sems.at[s]
        )
        copy.start()
        copies.append(copy)
    bits = share.bit_length() - 1
    live = jnp.where(valid_ref[...] > 0, 1.0, 0.0).astype(F32)
    owner = lax.broadcasted_iota(jnp.int32, (rows, frames), 0) >> bits
    hot = jnp.where(owner == lax.broadcasted_iota(jnp.int32, (rows, frames), 1), 1.0, 0.0)
    hot = hot.astype(BF)
    over = (((1,), (1,)), ((), ()))
    live_row = lax.dot_general(
        jnp.broadcast_to(live, (8, frames)).astype(BF), hot, over, preferred_element_type=F32
    )
    live_buf[...] = lax.dot_general(
        hot, jnp.broadcast_to(live, (size, frames)).astype(BF), over, preferred_element_type=F32
    )
    spans = video_rows(frames, share)
    masks = []
    for low, high in spans:
        n = high - low
        at_row = lax.broadcasted_iota(jnp.int32, (n, n), 0)
        at_col = lax.broadcasted_iota(jnp.int32, (n, n), 1)
        same_token = ((at_row ^ at_col) & (share - 1)) == 0
        allowed = same_token & ((live_row[0:1, low:high] > 0.5) | (at_row == at_col))
        masks.append(jnp.where(allowed, 0.0, LOW).astype(F32))
    outs = []
    for s in range(count):
        copies[s].wait()
        for (low, high), mask in zip(spans, masks):
            here = pl.ds(low, high - low)
            x = lax.dot_general(
                x_buf[s, here, 0:size],
                x_buf[s, here, size : 2 * size],
                over,
                preferred_element_type=F32,
            )
            x = x * scale + mask
            p = jnp.exp(x - jnp.max(x, axis=1, keepdims=True))
            total = jnp.sum(p, axis=1, keepdims=True)
            o = jnp.dot(
                p.astype(BF), x_buf[s, here, 2 * size : 3 * size], preferred_element_type=F32
            )
            out_buf[s, here, :] = (o / total * live_buf[here, :]).astype(BF)
        out = pltpu.make_async_copy(
            out_buf.at[s], out_ref.at[:, pl.ds(s * size, size)], out_sems.at[s]
        )
        out.start()
        outs.append(out)
    for out in outs:
        out.wait()


def temporal(x, valid_row, after, count, share, size, scale):
    rows = x.shape[0]
    return pl.pallas_call(
        functools.partial(temporal_kernel, scale, count, share),
        in_specs=[
            pl.BlockSpec(memory_space=pl.ANY),
            pl.BlockSpec(memory_space=pltpu.VMEM),
        ]
        + [pl.BlockSpec(memory_space=pl.ANY)] * len(after),
        out_specs=pl.BlockSpec(memory_space=pl.ANY),
        out_shape=jax.ShapeDtypeStruct((rows, count * size), BF),
        scratch_shapes=[
            pltpu.VMEM((count, rows, 3 * size), BF),
            pltpu.VMEM((count, rows, size), BF),
            pltpu.VMEM((rows, size), F32),
            pltpu.SemaphoreType.DMA((count,)),
            pltpu.SemaphoreType.DMA((count,)),
        ],
        compiler_params=params(),
        cost_estimate=pl.CostEstimate(
            flops=4 * rows * rows * size * count,
            bytes_accessed=8 * rows * size * count,
            transcendentals=rows * rows * count,
        ),
        name="temporal_heads",
    )(x, valid_row, *after)


def spatial_kernel(
    scale, tile, first, kind_ref, mask_ref, valid_ref, place_ref,
    q_ref, own_ref, before_ref, after_ref, out_ref
):
    heads = kind_ref.shape[0]
    head = head_at(first + pl.program_id(0), kind_ref, heads)
    tokens = q_ref.shape[0]
    tiles = tokens // tile
    frames = (before_ref, own_ref, after_ref)
    place = place_ref[0]
    last = valid_ref.shape[0] - 1
    near = [None, jnp.bool_(True), None]
    for o, there in ((0, jnp.maximum(place - 1, 0)), (2, jnp.minimum(place + 1, last))):
        same = ((there + SHIFT) // VIDEO == (place + SHIFT) // VIDEO) & (there != place)
        near[o] = same & (valid_ref[there] > 0)
    own_live = jnp.where(valid_ref[place] > 0, 1.0, 0.0).astype(F32)
    for i in range(tiles):
        rows = pl.ds(i * tile, tile)
        q = q_ref[rows, :]
        pieces = []
        for o in range(3):
            s = lax.dot_general(
                q, frames[o][:, 0:128], (((1,), (1,)), ((), ())), preferred_element_type=F32
            )
            for j in range(tiles):
                ok = (mask_ref[head, i, o * tiles + j] > 0) & near[o]
                low = jnp.where(ok, 0.0, LOW).astype(F32)
                pieces.append(s[:, j * tile : (j + 1) * tile] * scale + low)
        top = pieces[0]
        for x in pieces[1:]:
            top = jnp.maximum(top, x)
        top = jnp.max(top, axis=1, keepdims=True)
        pieces = [jnp.exp(x - top) for x in pieces]
        total = pieces[0]
        for x in pieces[1:]:
            total = total + x
        total = jnp.sum(total, axis=1, keepdims=True)
        o_sum = None
        for o in range(3):
            p = jnp.concatenate([x.astype(BF) for x in pieces[o * tiles : (o + 1) * tiles]], axis=1)
            part = jnp.dot(p, frames[o][:, 128:256], preferred_element_type=F32)
            o_sum = part if o_sum is None else o_sum + part
        out_ref[rows, :] = (o_sum / total * own_live).astype(BF)


def spatial(kind, mask, valid, place, q, own, before, after, first, count, channels, scale, tile):
    tokens = q.shape[0]
    heads = kind.shape[0]
    size = channels // heads

    def slot(i, *_):
        return (0, i)

    return pl.pallas_call(
        functools.partial(spatial_kernel, scale, tile, first),
        grid_spec=pltpu.PrefetchScalarGridSpec(
            num_scalar_prefetch=4,
            grid=(count,),
            in_specs=[pl.BlockSpec((tokens, size), slot)]
            + [pl.BlockSpec((tokens, 2 * size), slot)] * 3,
            out_specs=pl.BlockSpec(
                (tokens, size),
                lambda i, kind_ref, *_: (0, head_at(first + i, kind_ref, heads)),
            ),
        ),
        out_shape=jax.ShapeDtypeStruct((tokens, channels), BF),
        compiler_params=params(),
        cost_estimate=pl.CostEstimate(
            flops=12 * tokens * tokens * size * count,
            bytes_accessed=16 * tokens * size * count,
            transcendentals=3 * tokens * tokens * count,
        ),
        name="spatial_heads",
    )(kind, mask, valid, place, q, own, before, after)


def merge_kernel(count, kind_ref, base_ref, x_ref, out_ref, sems):
    heads = kind_ref.shape[0]
    size = out_ref.shape[1] // heads
    copies = []
    for s in range(count):
        start = pl.multiple_of(head_at(s, kind_ref, heads) * size, size)
        copy = pltpu.make_async_copy(
            x_ref.at[:, pl.ds(s * size, size)], out_ref.at[:, pl.ds(start, size)], sems.at[s]
        )
        copy.start()
        copies.append(copy)
    for copy in copies:
        copy.wait()


def merge(kind, base, x, count):
    return pl.pallas_call(
        functools.partial(merge_kernel, count),
        in_specs=[pl.BlockSpec(memory_space=pltpu.SMEM)]
        + [pl.BlockSpec(memory_space=pl.ANY)] * 2,
        out_specs=pl.BlockSpec(memory_space=pl.ANY),
        out_shape=jax.ShapeDtypeStruct(base.shape, BF),
        scratch_shapes=[pltpu.SemaphoreType.DMA((count,))],
        input_output_aliases={1: 0},
        compiler_params=params(),
        cost_estimate=pl.CostEstimate(flops=0, bytes_accessed=4 * x.size, transcendentals=0),
        name="merge_heads",
    )(kind, base, x)


def local(queries, keys, values, gain_q, gain_k, head_kind, tile_mask, frame_valid):
    heads = head_kind.shape[0]
    tokens, channels = queries.shape[1:]
    size = channels // heads
    tile = tokens // tile_mask.shape[1]
    frames = lax.axis_size("frames")
    blocks = lax.axis_size("heads")
    position = lax.axis_index("frames")
    scale = 1.0 / math.sqrt(size)
    share = tokens // frames
    q, k, v = queries[0], keys[0], values[0]

    parts = local_sums(q, k, blocks, tile)
    parts = lax.all_to_all(parts, "heads", split_axis=0, concat_axis=0, tiled=True)

    place = position[None]
    valid_row = frame_valid[None, :]
    up = [(i, i + 1) for i in range(frames - 1)]
    down = [(j, i) for i, j in up]

    def exchange(x):
        x = x.reshape(frames, share, x.shape[1])
        return lax.all_to_all(x, "frames", split_axis=0, concat_axis=0, tiled=True).reshape(
            tokens, x.shape[2]
        )

    def branch(count):
        rest = heads - count

        def run(q, k, v, parts):
            args = (head_kind, parts, gain_q, gain_k, q, k, v)
            (sent,) = pack(*args, 0, count, True, blocks * channels, tile)
            mine = exchange(sent)
            pair, near_q = pack(*args, count, rest, False, blocks * channels, tile)
            earlier = lax.ppermute(pair, "frames", up)
            later = lax.ppermute(pair, "frames", down)
            told = temporal(mine, valid_row, (earlier, later), count, share, size, scale)
            back = exchange(told)
            base = spatial(
                head_kind, tile_mask, frame_valid, place, near_q, pair, earlier, later,
                count, rest, channels, scale, tile,
            )
            return merge(head_kind, base, back, count)

        return run

    choice = jnp.sum(head_kind) - 1
    out = lax.switch(choice, [branch(c) for c in range(1, heads)], q, k, v, parts)
    return out[None]


def solution(mesh):
    placed = (
        P("frames", None, "heads"),
        P("frames", None, "heads"),
        P("frames", None, "heads"),
        P("heads"),
        P("heads"),
        P("heads"),
        P("heads", None, None),
        P(),
    )
    return jax.shard_map(
        local, mesh=mesh, in_specs=placed, out_specs=P("frames", None, "heads"), check_vma=False
    )
```

time: 165 us -> 161 us (0.976)
  between operations: 4.36 us -> 0.65 us
  Pallas kernels: 17.5 us -> 14.1 us
  starting transfers between devices: 40.1 us -> 43.5 us
  waiting for transfers between devices: 94.8 us -> 97.6 us
  local copies, waits for them, and re-layouts: 3.08 us -> 0.88 us
    all_to_all x2, waiting for transfers between devices: 71.5 us -> 26.8 us  [exchange(): lax.all_to_all(x, 'frames', split_axis=0, concat_axis=0, tiled=True)]
    ppermute x1, waiting for transfers between devices: 21.1 us -> 65.6 us  [run(): earlier = lax.ppermute(pair, 'frames', up)]
    pallas_call x5, Pallas kernels: 14.8 us -> 11.5 us  [the longest x2 4.79 us: pack(): pl.pallas_call(functools.partial(pack_kernel, all_channels, tile, first,...]
    all_to_all x2, starting transfers between devices: 25.8 us -> 29.1 us  [exchange(): lax.all_to_all(x, 'frames', split_axis=0, concat_axis=0, tiled=True)]
    all_to_all x1, waiting for transfers between devices: 0.01 us -> 2.78 us  [local(): lax.all_to_all(parts, 'heads', split_axis=0, concat_axis=0, tiled=True)]
  transfers between devices with their start and end apart: 5 -> 5, of which waited for: 3 -> 4; matrix products, arithmetic and copies ran while one was open for 2% -> 1% of each run, Pallas kernels for 3% -> 3%
where the time goes in v2:
time: 161 us; the launch traced here: 158 us
  waiting for transfers between devices  97.6 us (61%)
  starting transfers between devices  43.5 us (27%)
  Pallas kernels  14.1 us (9%)
    ppermute x1, waiting for transfers between devices, run(): earlier = lax.ppermute(pair, 'frames', up)  65.6 us
    all_to_all x2, starting transfers between devices, exchange(): lax.all_to_all(x, 'frames', split_axis=0, concat_axis=0, tiled=True)  29.1 us
    all_to_all x2, waiting for transfers between devices, exchange(): lax.all_to_all(x, 'frames', split_axis=0, concat_axis=0, tiled=True)  26.8 us
    all_to_all x1, starting transfers between devices, local(): lax.all_to_all(parts, 'heads', split_axis=0, concat_axis=0, tiled=True)  10.1 us
    pallas_call x2, Pallas kernels, pack(): pl.pallas_call(functools.partial(pack_kernel, all_channels, tile, first,...  4.79 us
    pallas_call x1, Pallas kernels, temporal(): pl.pallas_call(functools.partial(temporal_kernel, scale, count, share), i...  3.48 us
  transfers between devices with their start and end apart: 5, of which 4 were waited for; matrix products, arithmetic and copies ran while one was open for 1% of the time, Pallas kernels for 3%

profile of v2, /device:TPU:1, one launch (start us, length us, event | category | flops | bytes accessed | tf_op | source)
XLA Modules:
  0.0 158.3 jit_solution(2377309969115209223)
XLA Ops:
  0.0 2.5 %square_sums.1 = f32[8,8,128]{2,1,0:T(8,128)} custom-call(bf16[512,640]{1,0:T(8,128)(2,1)} %bitcast.42, bf16[512,640]{1,0:T(8,128)(2,1)} %bitcast.47), custom_call_target="tpu_custom_call" | custom-call | flops 1310720 | bytes 1310720 | tf_op jit(solution)/shard_map/square_sums/pallas_call | solution.py:61
  2.5 10.1 %all-to-all-start.8 = ((f32[8,8,128]{2,1,0:T(8,128)}), f32[8,8,128]{2,1,0:T(8,128)S(1)}, u32[]{:S(2)}, u32[]{:S(2)}) async-start(f32[8,8,128]{2,1,0:T(8,128)} %square_sums.1), calls=%async_computation.8 | async-start | bytes 65536 | tf_op jit(solution)/shard_map/all_to_all | solution.py:386
  12.7 1.3 reduce_sum.9
  14.6 2.8 %all-to-all-done.8 = f32[8,8,128]{2,1,0:T(8,128)S(1)} async-done(((f32[8,8,128]{2,1,0:T(8,128)}), f32[8,8,128]{2,1,0:T(8,128)S(1)}, u32[]{:S(2)}, u32[]{:S(2)}) %all-to-all-start.8) | async-done | bytes 32800 | tf_op jit(solution)/shard_map/all_to_all | solution.py:386
  17.4 140.9 %conditional.1 = (bf16[1,512,640]{2,1,0:T(8,128)(2,1)}) conditional(s32[]{:T(128)} %clamp.3, (s32[5]{0:T(128)}, f32[8,8,128]{2,1,0:T(8,128)S(1)}, f32[640]{0:T(1024)}, f32[640]{0:T(1024)}, bf16[512,640]{1,0:T(8,128)(2,1)}, /*index=5*/bf16[512,640]{1,0:T(8,128)(2,1)}, bf16[1,512,640]{2,1,0:T(8,128)(2,1)}, ...), branch_computations={%region_1.0_spmd, %region_2.0_spmd, %region_3.0_spmd, %region_4.0_... | conditional | flops 1746141184 | bytes 28333512 | solution.py:420
  17.4 3.2 %pack_temporal.7 = bf16[512,1536]{1,0:T(8,128)(2,1)} custom-call(s32[5]{0:T(128)} %get-tuple-element.138.kind_ref, f32[8,8,128]{2,1,0:T(8,128)S(1)} %get-tuple-element.142.parts_ref, f32[640]{0:T(1024)} %get-tuple-element.179.gq_ref, f32[640]{0:T(1024)} %get-tuple-element.183.gk_ref, bf16[512,640]{1,0:T(8,128)(2,1)} %get-tuple-element.145.q_ref, ...), custom_call_target="tpu_custom_call" | custom-call | flops 1048576 | bytes 3145728 | tf_op jit(solution)/shard_map/cond/branch_3_fun/pack_temporal/pallas_call | solution.py:143
  20.6 0.0 copy-start.5
  20.6 0.0 copy-start.14
  20.6 0.0 copy-start.18
  20.7 0.0 copy-start.22
  20.7 0.0 copy-start.26
  20.7 14.3 %all-to-all-start.6 = ((bf16[64,8,1536]{2,1,0:T(8,128)(2,1)}), bf16[64,8,1536]{2,1,0:T(8,128)(2,1)S(1)}, u32[]{:S(2)}, u32[]{:S(2)}) async-start(bf16[64,8,1536]{2,1,0:T(8,128)(2,1)} %bitcast.26), calls=%async_computation.6 | async-start | bytes 3145728 | tf_op jit(solution)/shard_map/cond/branch_3_fun/all_to_all | solution.py:395
  35.0 0.0 copy-start.30
  35.0 1.6 %pack_spatial.7 = (bf16[512,256]{1,0:T(8,128)(2,1)S(1)}, bf16[512,128]{1,0:T(8,128)(2,1)S(1)}) custom-call(s32[5]{0:T(128)S(1)} %copy-done.26, f32[8,8,128]{2,1,0:T(8,128)S(1)} %copy-done.14, f32[640]{0:T(1024)S(1)} %copy-done.18, f32[640]{0:T(1024)S(1)} %copy-done.22, bf16[512,640]{1,0:T(8,128)(2,1)S(1)} %copy-done.5, ...), custom_call_target="tpu_custom_call" | custom-call | flops 262144 | bytes 786432 | tf_op jit(solution)/shard_map/cond/branch_3_fun/pack_spatial/pallas_call | solution.py:143
  36.6 2.9 %collective-permute-start.6 = (bf16[512,256]{1,0:T(8,128)(2,1)S(1)}, bf16[512,256]{1,0:T(8,128)(2,1)S(1)}, u32[]{:S(2)}, u32[]{:S(2)}) collective-permute-start(bf16[512,256]{1,0:T(8,128)(2,1)S(1)} %get-tuple-element.149.own_ref), channel_id=1, source_target_pairs={{0,1},{1,2},{2,3},{3,4},{4,5},{5,6},{6,7},{7,8},{8,9},{9,10},{10,1... | collective-permute-start | bytes 786440 | tf_op jit(solution)/shard_map/cond/branch_3_fun/ppermute | solution.py:407
  39.6 1.3 collective-permute-start.7
  40.9 65.6 %collective-permute-done.6.before_ref.rest_0_ = bf16[512,256]{1,0:T(8,128)(2,1)S(1)} collective-permute-done((bf16[512,256]{1,0:T(8,128)(2,1)S(1)}, bf16[512,256]{1,0:T(8,128)(2,1)S(1)}, u32[]{:S(2)}, u32[]{:S(2)}) %collective-permute-start.6) | collective-permute-done | bytes 262176 | tf_op jit(solution)/shard_map/cond/branch_3_fun/ppermute | solution.py:407
  106.4 2.5 %collective-permute-done.7.after_ref.rest_1_ = bf16[512,256]{1,0:T(8,128)(2,1)S(1)} collective-permute-done((bf16[512,256]{1,0:T(8,128)(2,1)S(1)}, bf16[512,256]{1,0:T(8,128)(2,1)S(1)}, u32[]{:S(2)}, u32[]{:S(2)}) %collective-permute-start.7) | collective-permute-done | bytes 262176 | tf_op jit(solution)/shard_map/cond/branch_3_fun/ppermute | solution.py:408
  109.0 3.5 %temporal_heads.7 = bf16[512,512]{1,0:T(8,128)(2,1)} custom-call(bf16[512,1536]{1,0:T(8,128)(2,1)S(1)} %bitcast.34, s32[1,64]{1,0:T(1,128)S(1)} %bitcast.67, bf16[512,256]{1,0:T(8,128)(2,1)S(1)} %collective-permute-done.6.before_ref.rest_0_, bf16[512,256]{1,0:T(8,128)(2,1)S(1)} %collective-permute-done.7.after_ref.rest_1_), custom_call_target="tpu_custom_call" | custom-call | flops 536870912 | bytes 2097152 | tf_op jit(solution)/shard_map/cond/branch_3_fun/temporal_heads/pallas_call | solution.py:241
  112.5 14.8 %all-to-all-start.7 = ((bf16[64,8,512]{2,1,0:T(8,128)(2,1)}), bf16[64,8,512]{2,1,0:T(8,128)(2,1)S(1)}, u32[]{:S(2)}, u32[]{:S(2)}) async-start(bf16[64,8,512]{2,1,0:T(8,128)(2,1)} %bitcast.29), calls=%async_computation.7 | async-start | bytes 1048576 | tf_op jit(solution)/shard_map/cond/branch_3_fun/all_to_all | solution.py:395
  127.3 2.6 %spatial_heads.7.base_ref = bf16[512,640]{1,0:T(8,128)(2,1)S(1)} custom-call(s32[5]{0:T(128)S(1)} %copy-done.26, s32[5,4,12]{2,1,0:T(4,128)S(1)} %copy-done.32, s32[64]{0:T(128)S(1)} %copy-done.30, s32[1]{0:T(128)} %bitcast.24.place_ref, bf16[512,128]{1,0:T(8,128)(2,1)S(1)} %get-tuple-element.148.q_ref, bf16[512,256]{1,0:T(8,128)(2,1)S(1)} %get-tuple-element.149.own_ref, ...), custom_call_target="tpu_custom_call" | custom-call | flops 402653184 | bytes 1048576 | tf_op jit(solution)/shard_map/cond/branch_3_fun/spatial_heads/pallas_call | solution.py:320
  130.0 26.8 %all-to-all-done.7 = bf16[64,8,512]{2,1,0:T(8,128)(2,1)S(1)} async-done(((bf16[64,8,512]{2,1,0:T(8,128)(2,1)}), bf16[64,8,512]{2,1,0:T(8,128)(2,1)S(1)}, u32[]{:S(2)}, u32[]{:S(2)}) %all-to-all-start.7) | async-done | bytes 524320 | tf_op jit(solution)/shard_map/cond/branch_3_fun/all_to_all | solution.py:395
  156.7 0.7 merge_heads.7
  157.5 0.8 copy-done.9
  (12 shorter events, 0.0 us)
Async XLA Ops:
  2.5 14.9 %all-to-all-start.8 = ((f32[8,8,128]{2,1,0:T(8,128)}), f32[8,8,128]{2,1,0:T(8,128)S(1)}, u32[]{:S(2)}, u32[]{:S(2)}) async-start(f32[8,8,128]{2,1,0:T(8,128)} %square_sums.1), calls=%async_computation.8 | async-start | bytes 65536 | tf_op jit(solution)/shard_map/all_to_all | solution.py:386
  17.4 3.2 %copy-start.13 = (f32[8,8,128]{2,1,0:T(8,128)}, f32[8,8,128]{2,1,0:T(8,128)S(1)}, u32[]{:S(2)}) copy-start(f32[8,8,128]{2,1,0:T(8,128)S(1)} %get-tuple-element.142.parts_ref) | copy-start | bytes 98308 | tf_op jit(solution)/shard_map/cond
  20.6 14.3 %copy-start.5 = (bf16[512,640]{1,0:T(8,128)(2,1)S(1)}, bf16[512,640]{1,0:T(8,128)(2,1)}, u32[]{:S(2)}) copy-start(bf16[512,640]{1,0:T(8,128)(2,1)} %get-tuple-element.145.q_ref) | copy-start | bytes 1966084 | tf_op jit(solution)/shard_map/cond
  20.6 14.3 %copy-start.14 = (f32[8,8,128]{2,1,0:T(8,128)S(1)}, f32[8,8,128]{2,1,0:T(8,128)}, u32[]{:S(2)}) copy-start(f32[8,8,128]{2,1,0:T(8,128)} %copy-done.13) | copy-start | bytes 98308 | tf_op jit(solution)/shard_map/cond
  20.6 14.3 %copy-start.18 = (f32[640]{0:T(1024)S(1)}, f32[640]{0:T(1024)}, u32[]{:S(2)}) copy-start(f32[640]{0:T(1024)} %get-tuple-element.179.gq_ref) | copy-start | bytes 7684 | tf_op jit(solution)/shard_map/cond
  20.7 14.3 %copy-start.22 = (f32[640]{0:T(1024)S(1)}, f32[640]{0:T(1024)}, u32[]{:S(2)}) copy-start(f32[640]{0:T(1024)} %get-tuple-element.183.gk_ref) | copy-start | bytes 7684 | tf_op jit(solution)/shard_map/cond
  20.7 14.3 %copy-start.26 = (s32[5]{0:T(128)S(1)}, s32[5]{0:T(128)}, u32[]{:S(2)}) copy-start(s32[5]{0:T(128)} %get-tuple-element.138.kind_ref) | copy-start | bytes 64 | tf_op jit(solution)/shard_map/cond
  20.7 88.3 %all-to-all-start.6 = ((bf16[64,8,1536]{2,1,0:T(8,128)(2,1)}), bf16[64,8,1536]{2,1,0:T(8,128)(2,1)S(1)}, u32[]{:S(2)}, u32[]{:S(2)}) async-start(bf16[64,8,1536]{2,1,0:T(8,128)(2,1)} %bitcast.26), calls=%async_computation.6 | async-start | bytes 3145728 | tf_op jit(solution)/shard_map/cond/branch_3_fun/all_to_all | solution.py:395
  35.0 74.0 %copy-start.30 = (s32[64]{0:T(128)S(1)}, s32[64]{0:T(128)}, u32[]{:S(2)}) copy-start(s32[64]{0:T(128)} %get-tuple-element.175) | copy-start | bytes 772 | tf_op jit(solution)/shard_map/cond
  36.6 69.8 %collective-permute-start.6 = (bf16[512,256]{1,0:T(8,128)(2,1)S(1)}, bf16[512,256]{1,0:T(8,128)(2,1)S(1)}, u32[]{:S(2)}, u32[]{:S(2)}) collective-permute-start(bf16[512,256]{1,0:T(8,128)(2,1)S(1)} %get-tuple-element.149.own_ref), channel_id=1, source_target_pairs={{0,1},{1,2},{2,3},{3,4},{4,5},{5,6},{6,7},{7,8},{8,9},{9,10},{10,1... | collective-permute-start | bytes 786440 | tf_op jit(solution)/shard_map/cond/branch_3_fun/ppermute | solution.py:407
  39.6 69.4 %collective-permute-start.7 = (bf16[512,256]{1,0:T(8,128)(2,1)S(1)}, bf16[512,256]{1,0:T(8,128)(2,1)S(1)}, u32[]{:S(2)}, u32[]{:S(2)}) collective-permute-start(bf16[512,256]{1,0:T(8,128)(2,1)S(1)} %get-tuple-element.149.own_ref), channel_id=1, source_target_pairs={{1,0},{2,1},{3,2},{4,3},{5,4},{6,5},{7,6},{8,7},{9,8},{10,9},{11,1... | collective-permute-start | bytes 786440 | tf_op jit(solution)/shard_map/cond/branch_3_fun/ppermute | solution.py:408
  109.0 18.3 %copy-start.32 = (s32[5,4,12]{2,1,0:T(4,128)S(1)}, s32[5,4,12]{2,1,0:T(4,128)}, u32[]{:S(2)}) copy-start(s32[5,4,12]{2,1,0:T(4,128)} %get-tuple-element.191.mask_ref) | copy-start | bytes 2884 | tf_op jit(solution)/shard_map/cond
  112.5 44.3 %all-to-all-start.7 = ((bf16[64,8,512]{2,1,0:T(8,128)(2,1)}), bf16[64,8,512]{2,1,0:T(8,128)(2,1)S(1)}, u32[]{:S(2)}, u32[]{:S(2)}) async-start(bf16[64,8,512]{2,1,0:T(8,128)(2,1)} %bitcast.29), calls=%async_computation.7 | async-start | bytes 1048576 | tf_op jit(solution)/shard_map/cond/branch_3_fun/all_to_all | solution.py:395
  157.4 0.8 copy-start.9

commit v3 on v2

--- a/solution.py
+++ b/solution.py
@@ -78,28 +78,39 @@
     kind_ref, parts_ref, gq_ref, gk_ref, q_ref, k_ref, v_ref, *rest
 ):
     if joined:
-        out_ref, q_buf, k_buf, out_buf, rq, rk, in_sems, out_sems = rest
+        out_ref, q_buf, k_buf, out_buf, rq, rk, in_sems, out_sems = rest[-8:]
     else:
-        out_ref, qn_ref, q_buf, k_buf, out_buf, rq, rk, in_sems, out_sems = rest
+        out_ref, qn_ref, q_buf, k_buf, out_buf, rq, rk, in_sems, out_sems = rest[-9:]
     tokens = q_ref.shape[0]
     heads = kind_ref.shape[0]
     size = q_ref.shape[1] // heads
     width = out_buf.shape[2]
-    starts = []
-    copies = []
-    for s in range(count):
-        start = pl.multiple_of(head_at(first + s, kind_ref, heads) * size, size)
-        starts.append(start)
-        columns = pl.ds(start, size)
+
+    def column(s):
+        return pl.multiple_of(head_at(first + s, kind_ref, heads) * size, size)
+
+    def loads(s):
+        columns = pl.ds(column(s), size)
         trio = (
             (q_ref, q_buf.at[s]),
             (k_ref, k_buf.at[s]),
             (v_ref, out_buf.at[s, :, pl.ds(width - size, size)]),
         )
-        for n, (ref, buf) in enumerate(trio):
-            copy = pltpu.make_async_copy(ref.at[:, columns], buf, in_sems.at[3 * s + n])
+        return [
+            pltpu.make_async_copy(ref.at[:, columns], buf, in_sems.at[3 * s + n])
+            for n, (ref, buf) in enumerate(trio)
+        ]
+
+    def stores(s):
+        columns = pl.ds(pl.multiple_of(s * width, width), width)
+        return pltpu.make_async_copy(out_buf.at[s], out_ref.at[:, columns], out_sems.at[s])
+
+    def begin(s, carry):
+        for copy in loads(s):
             copy.start()
-            copies.append(copy)
+        return carry
+
+    lax.fori_loop(0, count, begin, 0)
     total = jnp.sum(parts_ref[...], axis=0)
     scale = lax.rsqrt(total / all_channels + epsilon)
     rows = tokens // tile
@@ -107,31 +118,36 @@
         here = pl.ds(c * tile, tile)
         rq[here, :] = jnp.broadcast_to(scale[c : c + 1, :], (tile, tile)).T
         rk[here, :] = jnp.broadcast_to(scale[rows + c : rows + c + 1, :], (tile, tile)).T
-    outs = []
-    for s in range(count):
-        gain_q = gq_ref[pl.ds(starts[s], size)].reshape(1, size)
-        gain_k = gk_ref[pl.ds(starts[s], size)].reshape(1, size)
-        copies[3 * s].wait()
+
+    def work(s, carry):
+        gain_q = gq_ref[pl.ds(column(s), size)].reshape(1, size)
+        gain_k = gk_ref[pl.ds(column(s), size)].reshape(1, size)
+        copies = loads(s)
+        copies[0].wait()
         normed_q = (q_buf[s].astype(F32) * rq[...] * gain_q).astype(BF)
-        copies[3 * s + 1].wait()
+        copies[1].wait()
         normed_k = (k_buf[s].astype(F32) * rk[...] * gain_k).astype(BF)
         if joined:
             out_buf[s, :, 0:size] = normed_q
             out_buf[s, :, size : 2 * size] = normed_k
         else:
-            qn_ref[:, s * size : (s + 1) * size] = normed_q
+            columns = pl.ds(pl.multiple_of(s * size, size), size)
+            qn_ref[:, columns] = normed_q
             out_buf[s, :, 0:size] = normed_k
-        copies[3 * s + 2].wait()
-        out = pltpu.make_async_copy(
-            out_buf.at[s], out_ref.at[:, pl.ds(s * width, width)], out_sems.at[s]
-        )
-        out.start()
-        outs.append(out)
-    for out in outs:
-        out.wait()
-
-
-def pack(kind, parts, gain_q, gain_k, q, k, v, first, count, joined, all_channels, tile):
+        copies[2].wait()
+        stores(s).start()
+        return carry
+
+    lax.fori_loop(0, count, work, 0)
+
+    def end(s, carry):
+        stores(s).wait()
+        return carry
+
+    lax.fori_loop(0, count, end, 0)
+
+
+def pack(kind, parts, gain_q, gain_k, q, k, v, after, first, count, joined, all_channels, tile):
     tokens, channels = q.shape
     size = channels // kind.shape[0]
     width = (3 if joined else 2) * size
@@ -144,7 +160,7 @@
         functools.partial(pack_kernel, all_channels, tile, first, count, joined),
         in_specs=[pl.BlockSpec(memory_space=pltpu.SMEM)]
         + [pl.BlockSpec(memory_space=pltpu.VMEM)] * 3
-        + [pl.BlockSpec(memory_space=pl.ANY)] * 3,
+        + [pl.BlockSpec(memory_space=pl.ANY)] * (3 + len(after)),
         out_specs=out_specs,
         out_shape=out_shape,
         scratch_shapes=[
@@ -163,7 +179,7 @@
             transcendentals=0,
         ),
         name="pack_temporal" if joined else "pack_spatial",
-    )(kind, parts, gain_q, gain_k, q, k, v)
+    )(kind, parts, gain_q, gain_k, q, k, v, *after)
 
 
 def video_rows(frames, share):
@@ -177,17 +193,22 @@
 
 
 def temporal_kernel(scale, count, share, x_ref, valid_ref, *rest):
-    out_ref, x_buf, out_buf, live_buf, in_sems, out_sems = rest[-6:]
+    spans = video_rows(valid_ref.shape[1], share)
+    out_ref, x_buf, out_buf, live_buf, *masks = rest[-6 - len(spans) : -2]
+    in_sems, out_sems = rest[-2:]
     rows = x_ref.shape[0]
     frames = valid_ref.shape[1]
     size = out_buf.shape[2]
-    copies = []
-    for s in range(count):
-        copy = pltpu.make_async_copy(
-            x_ref.at[:, pl.ds(s * 3 * size, 3 * size)], x_buf.at[s], in_sems.at[s]
-        )
-        copy.start()
-        copies.append(copy)
+
+    def load(s):
+        columns = pl.ds(pl.multiple_of(s * 3 * size, 3 * size), 3 * size)
+        return pltpu.make_async_copy(x_ref.at[:, columns], x_buf.at[s], in_sems.at[s])
+
+    def begin(s, carry):
+        load(s).start()
+        return carry
+
+    lax.fori_loop(0, count, begin, 0)
     bits = share.bit_length() - 1
     live = jnp.where(valid_ref[...] > 0, 1.0, 0.0).astype(F32)
     owner = lax.broadcasted_iota(jnp.int32, (rows, frames), 0) >> bits
@@ -200,18 +221,21 @@
     live_buf[...] = lax.dot_general(
         hot, jnp.broadcast_to(live, (size, frames)).astype(BF), over, preferred_element_type=F32
     )
-    spans = video_rows(frames, share)
-    masks = []
-    for low, high in spans:
+    for (low, high), mask in zip(spans, masks):
         n = high - low
         at_row = lax.broadcasted_iota(jnp.int32, (n, n), 0)
         at_col = lax.broadcasted_iota(jnp.int32, (n, n), 1)
         same_token = ((at_row ^ at_col) & (share - 1)) == 0
         allowed = same_token & ((live_row[0:1, low:high] > 0.5) | (at_row == at_col))
-        masks.append(jnp.where(allowed, 0.0, LOW).astype(F32))
-    outs = []
+        mask[...] = jnp.where(allowed, 0.0, LOW).astype(F32)
+
+    def store(s):
+        columns = pl.ds(pl.multiple_of(s * size, size), size)
+        return pltpu.make_async_copy(out_buf.at[s], out_ref.at[:, columns], out_sems.at[s])
+
     for s in range(count):
-        copies[s].wait()
+        load(s).wait()
+    for s in range(count):
         for (low, high), mask in zip(spans, masks):
             here = pl.ds(low, high - low)
             x = lax.dot_general(
@@ -220,20 +244,20 @@
                 over,
                 preferred_element_type=F32,
             )
-            x = x * scale + mask
-            p = jnp.exp(x - jnp.max(x, axis=1, keepdims=True))
+            x = x + mask[...]
+            p = jnp.exp2((x - jnp.max(x, axis=1, keepdims=True)) * scale)
             total = jnp.sum(p, axis=1, keepdims=True)
             o = jnp.dot(
                 p.astype(BF), x_buf[s, here, 2 * size : 3 * size], preferred_element_type=F32
             )
             out_buf[s, here, :] = (o / total * live_buf[here, :]).astype(BF)
-        out = pltpu.make_async_copy(
-            out_buf.at[s], out_ref.at[:, pl.ds(s * size, size)], out_sems.at[s]
-        )
-        out.start()
-        outs.append(out)
-    for out in outs:
-        out.wait()
+        store(s).start()
+
+    def end(s, carry):
+        store(s).wait()
+        return carry
+
+    lax.fori_loop(0, count, end, 0)
 
 
 def temporal(x, valid_row, after, count, share, size, scale):
@@ -251,6 +275,10 @@
             pltpu.VMEM((count, rows, 3 * size), BF),
             pltpu.VMEM((count, rows, size), BF),
             pltpu.VMEM((rows, size), F32),
+            *[
+                pltpu.VMEM((high - low, high - low), F32)
+                for low, high in video_rows(valid_row.shape[1], share)
+            ],
             pltpu.SemaphoreType.DMA((count,)),
             pltpu.SemaphoreType.DMA((count,)),
         ],
@@ -270,8 +298,8 @@
 ):
     heads = kind_ref.shape[0]
     head = head_at(first + pl.program_id(0), kind_ref, heads)
-    tokens = q_ref.shape[0]
-    tiles = tokens // tile
+    tiles = own_ref.shape[0] // tile
+    i = pl.program_id(1)
     frames = (before_ref, own_ref, after_ref)
     place = place_ref[0]
     last = valid_ref.shape[0] - 1
@@ -280,33 +308,31 @@
         same = ((there + SHIFT) // VIDEO == (place + SHIFT) // VIDEO) & (there != place)
         near[o] = same & (valid_ref[there] > 0)
     own_live = jnp.where(valid_ref[place] > 0, 1.0, 0.0).astype(F32)
-    for i in range(tiles):
-        rows = pl.ds(i * tile, tile)
-        q = q_ref[rows, :]
-        pieces = []
-        for o in range(3):
-            s = lax.dot_general(
-                q, frames[o][:, 0:128], (((1,), (1,)), ((), ())), preferred_element_type=F32
-            )
-            for j in range(tiles):
-                ok = (mask_ref[head, i, o * tiles + j] > 0) & near[o]
-                low = jnp.where(ok, 0.0, LOW).astype(F32)
-                pieces.append(s[:, j * tile : (j + 1) * tile] * scale + low)
-        top = pieces[0]
-        for x in pieces[1:]:
-            top = jnp.maximum(top, x)
-        top = jnp.max(top, axis=1, keepdims=True)
-        pieces = [jnp.exp(x - top) for x in pieces]
-        total = pieces[0]
-        for x in pieces[1:]:
-            total = total + x
-        total = jnp.sum(total, axis=1, keepdims=True)
-        o_sum = None
-        for o in range(3):
-            p = jnp.concatenate([x.astype(BF) for x in pieces[o * tiles : (o + 1) * tiles]], axis=1)
-            part = jnp.dot(p, frames[o][:, 128:256], preferred_element_type=F32)
-            o_sum = part if o_sum is None else o_sum + part
-        out_ref[rows, :] = (o_sum / total * own_live).astype(BF)
+    q = q_ref[...]
+    pieces = []
+    for o in range(3):
+        s = lax.dot_general(
+            q, frames[o][:, 0:128], (((1,), (1,)), ((), ())), preferred_element_type=F32
+        )
+        for j in range(tiles):
+            ok = (mask_ref[head, i, o * tiles + j] > 0) & near[o]
+            low = jnp.where(ok, 0.0, LOW).astype(F32)
+            pieces.append(s[:, j * tile : (j + 1) * tile] + low)
+    top = pieces[0]
+    for x in pieces[1:]:
+        top = jnp.maximum(top, x)
+    top = jnp.max(top, axis=1, keepdims=True)
+    pieces = [jnp.exp2((x - top) * scale) for x in pieces]
+    total = pieces[0]
+    for x in pieces[1:]:
+        total = total + x
+    total = jnp.sum(total, axis=1, keepdims=True)
+    o_sum = None
+    for o in range(3):
+        p = jnp.concatenate([x.astype(BF) for x in pieces[o * tiles : (o + 1) * tiles]], axis=1)
+        part = jnp.dot(p, frames[o][:, 128:256], preferred_element_type=F32)
+        o_sum = part if o_sum is None else o_sum + part
+    out_ref[...] = (o_sum / total * own_live).astype(BF)
 
 
 def spatial(kind, mask, valid, place, q, own, before, after, first, count, channels, scale, tile):
@@ -314,19 +340,19 @@
     heads = kind.shape[0]
     size = channels // heads
 
-    def slot(i, *_):
+    def slot(i, j, *_):
         return (0, i)
 
     return pl.pallas_call(
         functools.partial(spatial_kernel, scale, tile, first),
         grid_spec=pltpu.PrefetchScalarGridSpec(
             num_scalar_prefetch=4,
-            grid=(count,),
-            in_specs=[pl.BlockSpec((tokens, size), slot)]
+            grid=(count, tokens // tile),
+            in_specs=[pl.BlockSpec((tile, size), lambda i, j, *_: (j, i))]
             + [pl.BlockSpec((tokens, 2 * size), slot)] * 3,
             out_specs=pl.BlockSpec(
-                (tokens, size),
-                lambda i, kind_ref, *_: (0, head_at(first + i, kind_ref, heads)),
+                (tile, size),
+                lambda i, j, kind_ref, *_: (j, head_at(first + i, kind_ref, heads)),
             ),
         ),
         out_shape=jax.ShapeDtypeStruct((tokens, channels), BF),
@@ -359,8 +385,8 @@
     return pl.pallas_call(
         functools.partial(merge_kernel, count),
         in_specs=[pl.BlockSpec(memory_space=pltpu.SMEM)]
-        + [pl.BlockSpec(memory_space=pl.ANY)] * 2,
-        out_specs=pl.BlockSpec(memory_space=pl.ANY),
+        + [pl.BlockSpec(memory_space=pltpu.HBM), pl.BlockSpec(memory_space=pl.ANY)],
+        out_specs=pl.BlockSpec(memory_space=pltpu.HBM),
         out_shape=jax.ShapeDtypeStruct(base.shape, BF),
         scratch_shapes=[pltpu.SemaphoreType.DMA((count,))],
         input_output_aliases={1: 0},
@@ -378,7 +404,7 @@
     frames = lax.axis_size("frames")
     blocks = lax.axis_size("heads")
     position = lax.axis_index("frames")
-    scale = 1.0 / math.sqrt(size)
+    scale = math.log2(math.e) / math.sqrt(size)
     share = tokens // frames
     q, k, v = queries[0], keys[0], values[0]
 
@@ -396,28 +422,55 @@
             tokens, x.shape[2]
         )
 
-    def branch(count):
+    def branch(count, late):
         rest = heads - count
 
         def run(q, k, v, parts):
             args = (head_kind, parts, gain_q, gain_k, q, k, v)
-            (sent,) = pack(*args, 0, count, True, blocks * channels, tile)
-            mine = exchange(sent)
-            pair, near_q = pack(*args, count, rest, False, blocks * channels, tile)
-            earlier = lax.ppermute(pair, "frames", up)
-            later = lax.ppermute(pair, "frames", down)
-            told = temporal(mine, valid_row, (earlier, later), count, share, size, scale)
+
+            def near():
+                pair, near_q = pack(*args, (), count, rest, False, blocks * channels, tile)
+                earlier = lax.ppermute(pair, "frames", up)
+                later = lax.ppermute(pair, "frames", down)
+                return near_q, pair, earlier, later
+
+            def attend(near_q, pair, earlier, later):
+                return spatial(
+                    head_kind, tile_mask, frame_valid, place, near_q, pair, earlier, later,
+                    count, rest, channels, scale, tile,
+                )
+
+            def send(*after):
+                (sent,) = pack(*args, after, 0, count, True, blocks * channels, tile)
+                return exchange(sent)
+
+            if late == 0:
+                mine = send()
+                found = near()
+                after = found[2:]
+            elif late == 1:
+                found = near()
+                mine = send(*found[2:])
+                after = ()
+            else:
+                found = near()
+                base = attend(*found)
+                mine = send(base)
+                after = ()
+            told = temporal(mine, valid_row, after, count, share, size, scale)
             back = exchange(told)
-            base = spatial(
-                head_kind, tile_mask, frame_valid, place, near_q, pair, earlier, later,
-                count, rest, channels, scale, tile,
-            )
+            if late < 2:
+                base = attend(*found)
             return merge(head_kind, base, back, count)
 
         return run
 
-    choice = jnp.sum(head_kind) - 1
-    out = lax.switch(choice, [branch(c) for c in range(1, heads)], q, k, v, parts)
+    count = jnp.sum(head_kind)
+    odd = lax.axis_index("heads") % 2
+    choice = count - 1 + jnp.where((odd == 1) & (count > 2), heads - 3, 0)
+    branches = [branch(c, 0) for c in range(1, heads)]
+    branches += [branch(c, 2) for c in range(3, heads)]
+    out = lax.switch(choice, branches, q, k, v, parts)
     return out[None]
 
 

time: 161 us -> 151 us (0.938); the launches traced: 158 us -> 150 us
  blocking collectives: 0 us -> 112 us
  waiting for transfers between devices: 97.6 us -> 7.68 us
  starting transfers between devices: 43.5 us -> 13 us
    all_to_all x0 -> x2, blocking collectives: none -> 112 us  [exchange(): lax.all_to_all(x, 'frames', split_axis=0, concat_axis=0, tiled=True)]
    ppermute x2, waiting for transfers between devices: 68.1 us -> 5.56 us  [the longest x1 3.83 us: near(): later = lax.ppermute(pair, 'frames', down)]
    all_to_all x2 -> x0, starting transfers between devices: 29.1 us -> none  [exchange(): lax.all_to_all(x, 'frames', split_axis=0, concat_axis=0, tiled=True)]
    all_to_all x2 -> x0, waiting for transfers between devices: 26.8 us -> none  [exchange(): lax.all_to_all(x, 'frames', split_axis=0, concat_axis=0, tiled=True)]
  transfers between devices with their start and end apart: 5 -> 3, of which waited for: 4 -> 3; matrix products, arithmetic and copies ran while one was open for 1% -> 1% of each run, Pallas kernels for 3% -> 0%
where the time goes in v3:
time: 151 us; the launch traced here: 150 us
  blocking collectives  112 us (74%)
  Pallas kernels  13.4 us (9%)
  starting transfers between devices  13 us (9%)
  waiting for transfers between devices  7.68 us (5%)
    all_to_all x2, blocking collectives, exchange(): lax.all_to_all(x, 'frames', split_axis=0, concat_axis=0, tiled=True)  112 us
    all_to_all x1, starting transfers between devices, local(): lax.all_to_all(parts, 'heads', split_axis=0, concat_axis=0, tiled=True)  10.1 us
    ppermute x1, waiting for transfers between devices, near(): later = lax.ppermute(pair, 'frames', down)  3.83 us
    pallas_call x2, Pallas kernels, pack(): pl.pallas_call(functools.partial(pack_kernel, all_channels, tile, first,...  3.81 us
    pallas_call x1, Pallas kernels, spatial(): pl.pallas_call(functools.partial(spatial_kernel, scale, tile, first), gri...  3.32 us
  transfers between devices with their start and end apart: 3, of which 3 were waited for; matrix products, arithmetic and copies ran while one was open for 1% of the time, Pallas kernels for 0%

profile of v3, /device:TPU:1, one launch (start us, length us, event | category | flops | bytes accessed | tf_op | source)
XLA Modules:
  0.0 150.0 jit_solution(9629561985687372050)
XLA Ops:
  0.0 2.5 %square_sums.1 = f32[8,8,128]{2,1,0:T(8,128)} custom-call(bf16[512,640]{1,0:T(8,128)(2,1)} %bitcast.66, bf16[512,640]{1,0:T(8,128)(2,1)} %bitcast.73), custom_call_target="tpu_custom_call" | custom-call | flops 1310720 | bytes 1310720 | tf_op jit(solution)/shard_map/square_sums/pallas_call | solution.py:61
  2.5 10.1 %all-to-all-start.12 = ((f32[8,8,128]{2,1,0:T(8,128)}), f32[8,8,128]{2,1,0:T(8,128)S(1)}, u32[]{:S(2)}, u32[]{:S(2)}) async-start(f32[8,8,128]{2,1,0:T(8,128)} %square_sums.1), calls=%async_computation.12 | async-start | bytes 65536 | tf_op jit(solution)/shard_map/all_to_all | solution.py:412
  12.7 1.4 reduce_sum.9
  15.3 2.1 %all-to-all-done.12 = f32[8,8,128]{2,1,0:T(8,128)S(1)} async-done(((f32[8,8,128]{2,1,0:T(8,128)}), f32[8,8,128]{2,1,0:T(8,128)S(1)}, u32[]{:S(2)}, u32[]{:S(2)}) %all-to-all-start.12) | async-done | bytes 32800 | tf_op jit(solution)/shard_map/all_to_all | solution.py:412
  17.4 132.5 %conditional.1 = (bf16[1,512,640]{2,1,0:T(8,128)(2,1)}) conditional(s32[]{:T(128)} %clamp.3, (s32[5]{0:T(128)}, f32[8,8,128]{2,1,0:T(8,128)S(1)}, f32[640]{0:T(1024)}, f32[640]{0:T(1024)}, bf16[512,640]{1,0:T(8,128)(2,1)}, /*index=5*/bf16[512,640]{1,0:T(8,128)(2,1)}, bf16[1,512,640]{2,1,0:T(8,128)(2,1)}, ...), branch_computations={%region_1.2_spmd, %region_2.3_spmd, %region_3.4_spmd, %region_4.5_... | conditional | flops 1746141184 | bytes 28333512 | solution.py:473
  17.4 0.0 copy-start.11
  17.4 0.0 copy-start.13
  17.4 0.0 copy-start.28
  17.5 0.0 copy-start.34
  17.5 2.0 %pack_spatial.11 = (bf16[512,256]{1,0:T(8,128)(2,1)S(1)}, bf16[512,128]{1,0:T(8,128)(2,1)S(1)}) custom-call(s32[5]{0:T(128)} %get-tuple-element.210.kind_ref, f32[8,8,128]{2,1,0:T(8,128)S(1)} %get-tuple-element.214.parts_ref, f32[640]{0:T(1024)} %get-tuple-element.265.gq_ref, f32[640]{0:T(1024)} %get-tuple-element.271.gk_ref, ...), custom_call_target="tpu_custom_call" | custom-call | flops 262144 | bytes 786432 | tf_op jit(solution)/shard_map/cond/branch_5_fun/pack_spatial/pallas_call | solution.py:159
  19.4 1.3 collective-permute-start.10
  20.8 1.6 %collective-permute-start.11 = (bf16[512,256]{1,0:T(8,128)(2,1)S(1)}, bf16[512,256]{1,0:T(8,128)(2,1)S(1)}, u32[]{:S(2)}, u32[]{:S(2)}) collective-permute-start(bf16[512,256]{1,0:T(8,128)(2,1)S(1)} %get-tuple-element.221.own_ref), channel_id=1, source_target_pairs={{1,0},{2,1},{3,2},{4,3},{5,4},{6,5},{7,6},{8,7},{9,8},{10,9},{11,1... | collective-permute-start | bytes 786440 | tf_op jit(solution)/shard_map/cond/branch_5_fun/ppermute | solution.py:434
  22.3 1.7 %collective-permute-done.10.before_ref = bf16[512,256]{1,0:T(8,128)(2,1)S(1)} collective-permute-done((bf16[512,256]{1,0:T(8,128)(2,1)S(1)}, bf16[512,256]{1,0:T(8,128)(2,1)S(1)}, u32[]{:S(2)}, u32[]{:S(2)}) %collective-permute-start.10) | collective-permute-done | bytes 262176 | tf_op jit(solution)/shard_map/cond/branch_5_fun/ppermute | solution.py:433
  24.0 3.8 %collective-permute-done.11.after_ref = bf16[512,256]{1,0:T(8,128)(2,1)S(1)} collective-permute-done((bf16[512,256]{1,0:T(8,128)(2,1)S(1)}, bf16[512,256]{1,0:T(8,128)(2,1)S(1)}, u32[]{:S(2)}, u32[]{:S(2)}) %collective-permute-start.11) | collective-permute-done | bytes 262176 | tf_op jit(solution)/shard_map/cond/branch_5_fun/ppermute | solution.py:434
  27.9 0.0 copy-done.40
  27.9 0.0 copy-done.44
  27.9 3.3 %spatial_heads.11.rest_0_.base_ref = bf16[512,640]{1,0:T(8,128)(2,1)S(1)} custom-call(s32[5]{0:T(128)S(1)} %copy-done.40, s32[5,4,12]{2,1,0:T(4,128)S(1)} %copy-done.44, s32[64]{0:T(128)S(1)} %copy-done.50, s32[1]{0:T(128)} %bitcast.40.place_ref, bf16[512,128]{1,0:T(8,128)(2,1)S(1)} %get-tuple-element.220.q_ref, ...), custom_call_target="tpu_custom_call" | custom-call | flops 402653184 | bytes 1048576 | tf_op jit(solution)/shard_map/cond/branch_5_fun/spatial_heads/pallas_call | solution.py:346
  31.3 1.9 %pack_temporal.11 = bf16[512,1536]{1,0:T(8,128)(2,1)S(1)} custom-call(s32[5]{0:T(128)S(1)} %copy-done.40, f32[8,8,128]{2,1,0:T(8,128)S(1)} %get-tuple-element.214.parts_ref, f32[640]{0:T(1024)S(1)} %copy-done.28, f32[640]{0:T(1024)S(1)} %copy-done.34, bf16[512,640]{1,0:T(8,128)(2,1)S(1)} %copy-done.7, bf16[512,640]{1,0:T(8,128)(2,1)S(1)} %copy-done.11, ...), custom_call_target="tpu_custom_call" | custom-call | flops 1048576 | bytes 3145728 | tf_op jit(solution)/shard_map/cond/branch_5_fun/pack_temporal/pallas_call | solution.py:159
  33.1 77.0 %all_to_all.55 = bf16[64,8,1536]{2,1,0:T(8,128)(2,1)S(1)} all-to-all(bf16[64,8,1536]{2,1,0:T(8,128)(2,1)S(1)} %bitcast.52), channel_id=1, replica_groups=mesh['heads'=8,'frames'=64] {'frames'}, dimensions={0} | all-to-all | bytes 3145728 | tf_op jit(solution)/shard_map/cond/branch_5_fun/all_to_all | solution.py:421
  110.1 3.0 %temporal_heads.11 = bf16[512,512]{1,0:T(8,128)(2,1)S(1)} custom-call(bf16[512,1536]{1,0:T(8,128)(2,1)S(1)} %bitcast.51, s32[1,64]{1,0:T(1,128)S(1)} %bitcast.103), custom_call_target="tpu_custom_call" | custom-call | flops 536870912 | bytes 2097152 | tf_op jit(solution)/shard_map/cond/branch_5_fun/temporal_heads/pallas_call | solution.py:265
  113.1 35.3 %all_to_all.56 = bf16[64,8,512]{2,1,0:T(8,128)(2,1)S(1)} all-to-all(bf16[64,8,512]{2,1,0:T(8,128)(2,1)S(1)} %bitcast.57), channel_id=1, replica_groups=mesh['heads'=8,'frames'=64] {'frames'}, dimensions={0} | all-to-all | bytes 1048576 | tf_op jit(solution)/shard_map/cond/branch_5_fun/all_to_all | solution.py:421
  148.4 0.7 merge_heads.11
  149.1 0.0 copy-start.17
  149.1 0.8 copy-done.17
  (10 shorter events, 0.0 us)
Async XLA Ops:
  2.5 14.9 %all-to-all-start.12 = ((f32[8,8,128]{2,1,0:T(8,128)}), f32[8,8,128]{2,1,0:T(8,128)S(1)}, u32[]{:S(2)}, u32[]{:S(2)}) async-start(f32[8,8,128]{2,1,0:T(8,128)} %square_sums.1), calls=%async_computation.12 | async-start | bytes 65536 | tf_op jit(solution)/shard_map/all_to_all | solution.py:412
  17.4 10.5 %copy-start.40 = (s32[5]{0:T(128)S(1)}, s32[5]{0:T(128)}, u32[]{:S(2)}) copy-start(s32[5]{0:T(128)} %get-tuple-element.210.kind_ref) | copy-start | bytes 64 | tf_op jit(solution)/shard_map/cond
  17.4 10.5 %copy-start.44 = (s32[5,4,12]{2,1,0:T(4,128)S(1)}, s32[5,4,12]{2,1,0:T(4,128)}, u32[]{:S(2)}) copy-start(s32[5,4,12]{2,1,0:T(4,128)} %get-tuple-element.283.mask_ref) | copy-start | bytes 2884 | tf_op jit(solution)/shard_map/cond
  17.4 10.5 %copy-start.50 = (s32[64]{0:T(128)S(1)}, s32[64]{0:T(128)}, u32[]{:S(2)}) copy-start(s32[64]{0:T(128)} %get-tuple-element.259) | copy-start | bytes 772 | tf_op jit(solution)/shard_map/cond
  17.4 13.8 %copy-start.7 = (bf16[512,640]{1,0:T(8,128)(2,1)S(1)}, bf16[512,640]{1,0:T(8,128)(2,1)}, u32[]{:S(2)}) copy-start(bf16[512,640]{1,0:T(8,128)(2,1)} %get-tuple-element.217.q_ref) | copy-start | bytes 1966084 | tf_op jit(solution)/shard_map/cond
  17.4 13.8 %copy-start.11 = (bf16[512,640]{1,0:T(8,128)(2,1)S(1)}, bf16[512,640]{1,0:T(8,128)(2,1)}, u32[]{:S(2)}) copy-start(bf16[512,640]{1,0:T(8,128)(2,1)} %get-tuple-element.218.k_ref) | copy-start | bytes 1966084 | tf_op jit(solution)/shard_map/cond
  17.4 13.8 %copy-start.13 = (bf16[1,512,640]{2,1,0:T(8,128)(2,1)S(1)}, bf16[1,512,640]{2,1,0:T(8,128)(2,1)}, u32[]{:S(2)}) copy-start(bf16[1,512,640]{2,1,0:T(8,128)(2,1)} %get-tuple-element.289) | copy-start | bytes 1966084 | tf_op jit(solution)/shard_map/cond
  17.4 13.8 %copy-start.28 = (f32[640]{0:T(1024)S(1)}, f32[640]{0:T(1024)}, u32[]{:S(2)}) copy-start(f32[640]{0:T(1024)} %get-tuple-element.265.gq_ref) | copy-start | bytes 7684 | tf_op jit(solution)/shard_map/cond
  17.5 13.8 %copy-start.34 = (f32[640]{0:T(1024)S(1)}, f32[640]{0:T(1024)}, u32[]{:S(2)}) copy-start(f32[640]{0:T(1024)} %get-tuple-element.271.gk_ref) | copy-start | bytes 7684 | tf_op jit(solution)/shard_map/cond
  19.4 4.6 %collective-permute-start.10 = (bf16[512,256]{1,0:T(8,128)(2,1)S(1)}, bf16[512,256]{1,0:T(8,128)(2,1)S(1)}, u32[]{:S(2)}, u32[]{:S(2)}) collective-permute-start(bf16[512,256]{1,0:T(8,128)(2,1)S(1)} %get-tuple-element.221.own_ref), channel_id=1, source_target_pairs={{0,1},{1,2},{2,3},{3,4},{4,5},{5,6},{6,7},{7,8},{8,9},{9,10},{10,1... | collective-permute-start | bytes 786440 | tf_op jit(solution)/shard_map/cond/branch_5_fun/ppermute | solution.py:433
  20.8 7.1 %collective-permute-start.11 = (bf16[512,256]{1,0:T(8,128)(2,1)S(1)}, bf16[512,256]{1,0:T(8,128)(2,1)S(1)}, u32[]{:S(2)}, u32[]{:S(2)}) collective-permute-start(bf16[512,256]{1,0:T(8,128)(2,1)S(1)} %get-tuple-element.221.own_ref), channel_id=1, source_target_pairs={{1,0},{2,1},{3,2},{4,3},{5,4},{6,5},{7,6},{8,7},{9,8},{10,9},{11,1... | collective-permute-start | bytes 786440 | tf_op jit(solution)/shard_map/cond/branch_5_fun/ppermute | solution.py:434
  149.1 0.8 copy-start.17

commit v4 on v3

--- a/solution.py
+++ b/solution.py
@@ -447,7 +447,7 @@
             if late == 0:
                 mine = send()
                 found = near()
-                after = found[2:]
+                after = found[1:2]
             elif late == 1:
                 found = near()
                 mine = send(*found[2:])

time: 151 us -> 137 us (0.907)
  the two profiles are of different devices: /device:TPU:1 before, /device:TPU:5 now
where the time goes in v4:
time: 137 us; the launch traced here: 136 us
  blocking collectives  95.7 us (70%)
  Pallas kernels  15.7 us (11%)
  starting transfers between devices  12.2 us (9%)
  waiting for transfers between devices  8.63 us (6%)
    all_to_all x2, blocking collectives, exchange(): lax.all_to_all(x, 'frames', split_axis=0, concat_axis=0, tiled=True)  95.7 us
    all_to_all x1, starting transfers between devices, local(): lax.all_to_all(parts, 'heads', split_axis=0, concat_axis=0, tiled=True)  9.47 us
    pallas_call x1, Pallas kernels, spatial(): pl.pallas_call(functools.partial(spatial_kernel, scale, tile, first), gri...  6.43 us
    ppermute x1, waiting for transfers between devices, near(): earlier = lax.ppermute(pair, 'frames', up)  4.78 us
    ppermute x1, waiting for transfers between devices, near(): later = lax.ppermute(pair, 'frames', down)  3.85 us
    pallas_call x2, Pallas kernels, pack(): pl.pallas_call(functools.partial(pack_kernel, all_channels, tile, first,...  3.72 us
  transfers between devices with their start and end apart: 3, of which 2 were waited for; matrix products, arithmetic and copies ran while one was open for 1% of the time, Pallas kernels for 0%

profile of v4, /device:TPU:5, one launch (start us, length us, event | category | flops | bytes accessed | tf_op | source)
XLA Modules:
  0.0 136.2 jit_solution(14817959322580790053)
XLA Ops:
  0.0 2.5 %square_sums.1 = f32[8,8,128]{2,1,0:T(8,128)} custom-call(bf16[512,640]{1,0:T(8,128)(2,1)} %bitcast.66, bf16[512,640]{1,0:T(8,128)(2,1)} %bitcast.73), custom_call_target="tpu_custom_call" | custom-call | flops 1310720 | bytes 1310720 | tf_op jit(solution)/shard_map/square_sums/pallas_call | solution.py:61
  2.5 9.5 %all-to-all-start.12 = ((f32[8,8,128]{2,1,0:T(8,128)}), f32[8,8,128]{2,1,0:T(8,128)S(1)}, u32[]{:S(2)}, u32[]{:S(2)}) async-start(f32[8,8,128]{2,1,0:T(8,128)} %square_sums.1), calls=%async_computation.12 | async-start | bytes 65536 | tf_op jit(solution)/shard_map/all_to_all | solution.py:412
  12.0 1.4 reduce_sum.9
  14.7 121.6 %conditional.1 = (bf16[1,512,640]{2,1,0:T(8,128)(2,1)}) conditional(s32[]{:T(128)} %clamp.3, (s32[5]{0:T(128)}, f32[8,8,128]{2,1,0:T(8,128)S(1)}, f32[640]{0:T(1024)}, f32[640]{0:T(1024)}, bf16[512,640]{1,0:T(8,128)(2,1)}, /*index=5*/bf16[512,640]{1,0:T(8,128)(2,1)}, bf16[1,512,640]{2,1,0:T(8,128)(2,1)}, ...), branch_computations={%region_1.2_spmd, %region_2.3_spmd, %region_3.4_spmd, %region_4.5_... | conditional | flops 1746141184 | bytes 28333512 | solution.py:473
  14.9 0.0 copy-start.43
  14.9 0.0 copy-start.48
  15.0 0.0 copy-start.54
  15.0 2.1 %pack_spatial.10 = (bf16[512,512]{1,0:T(8,128)(2,1)S(1)}, bf16[512,256]{1,0:T(8,128)(2,1)S(1)}) custom-call(s32[5]{0:T(128)} %get-tuple-element.197.kind_ref, f32[8,8,128]{2,1,0:T(8,128)S(1)} %get-tuple-element.201.parts_ref, f32[640]{0:T(1024)} %get-tuple-element.264.gq_ref, f32[640]{0:T(1024)} %get-tuple-element.270.gk_ref, ...), custom_call_target="tpu_custom_call" | custom-call | flops 524288 | bytes 1572864 | tf_op jit(solution)/shard_map/cond/branch_4_fun/pack_spatial/pallas_call | solution.py:159
  17.1 0.0 copy-start.6
  17.1 0.0 copy-start.12
  17.1 0.0 copy-start.14
  17.2 0.0 copy-start.31
  17.2 0.0 copy-start.37
  17.2 1.5 %collective-permute-start.8 = (bf16[512,512]{1,0:T(8,128)(2,1)S(1)}, bf16[512,512]{1,0:T(8,128)(2,1)S(1)}, u32[]{:S(2)}, u32[]{:S(2)}) collective-permute-start(bf16[512,512]{1,0:T(8,128)(2,1)S(1)} %get-tuple-element.208.own_ref), channel_id=1, source_target_pairs={{0,1},{1,2},{2,3},{3,4},{4,5},{5,6},{6,7},{7,8},{8,9},{9,10},{10,1... | collective-permute-start | bytes 1572872 | tf_op jit(solution)/shard_map/cond/branch_4_fun/ppermute | solution.py:433
  18.6 1.3 collective-permute-start.9
  19.9 4.8 %collective-permute-done.8.before_ref = bf16[512,512]{1,0:T(8,128)(2,1)S(1)} collective-permute-done((bf16[512,512]{1,0:T(8,128)(2,1)S(1)}, bf16[512,512]{1,0:T(8,128)(2,1)S(1)}, u32[]{:S(2)}, u32[]{:S(2)}) %collective-permute-start.8) | collective-permute-done | bytes 524320 | tf_op jit(solution)/shard_map/cond/branch_4_fun/ppermute | solution.py:433
  24.7 3.8 %collective-permute-done.9.after_ref = bf16[512,512]{1,0:T(8,128)(2,1)S(1)} collective-permute-done((bf16[512,512]{1,0:T(8,128)(2,1)S(1)}, bf16[512,512]{1,0:T(8,128)(2,1)S(1)}, u32[]{:S(2)}, u32[]{:S(2)}) %collective-permute-start.9) | collective-permute-done | bytes 524320 | tf_op jit(solution)/shard_map/cond/branch_4_fun/ppermute | solution.py:434
  28.6 6.4 %spatial_heads.10.rest_0_.base_ref = bf16[512,640]{1,0:T(8,128)(2,1)S(1)} custom-call(s32[5]{0:T(128)S(1)} %copy-done.43, s32[5,4,12]{2,1,0:T(4,128)S(1)} %copy-done.48, s32[64]{0:T(128)S(1)} %copy-done.54, s32[1]{0:T(128)} %bitcast.32.place_ref, bf16[512,256]{1,0:T(8,128)(2,1)S(1)} %get-tuple-element.207.q_ref, ...), custom_call_target="tpu_custom_call" | custom-call | flops 805306368 | bytes 2097152 | tf_op jit(solution)/shard_map/cond/branch_4_fun/spatial_heads/pallas_call | solution.py:346
  35.1 1.6 %pack_temporal.10 = bf16[512,1152]{1,0:T(8,128)(2,1)S(1)} custom-call(s32[5]{0:T(128)S(1)} %copy-done.43, f32[8,8,128]{2,1,0:T(8,128)S(1)} %get-tuple-element.201.parts_ref, f32[640]{0:T(1024)S(1)} %copy-done.31, f32[640]{0:T(1024)S(1)} %copy-done.37, bf16[512,640]{1,0:T(8,128)(2,1)S(1)} %copy-done.6, bf16[512,640]{1,0:T(8,128)(2,1)S(1)} %copy-done.12, ...), custom_call_target="tpu_custom_call" | custom-call | flops 786432 | bytes 2359296 | tf_op jit(solution)/shard_map/cond/branch_4_fun/pack_temporal/pallas_call | solution.py:159
  36.6 64.1 %all_to_all.53 = bf16[64,8,1152]{2,1,0:T(8,128)(2,1)S(1)} all-to-all(bf16[64,8,1152]{2,1,0:T(8,128)(2,1)S(1)} %bitcast.55), channel_id=1, replica_groups=mesh['heads'=8,'frames'=64] {'frames'}, dimensions={0} | all-to-all | bytes 2359296 | tf_op jit(solution)/shard_map/cond/branch_4_fun/all_to_all | solution.py:421
  100.7 2.4 %temporal_heads.10 = bf16[512,384]{1,0:T(8,128)(2,1)S(1)} custom-call(bf16[512,1152]{1,0:T(8,128)(2,1)S(1)} %bitcast.54, s32[1,64]{1,0:T(1,128)S(1)} %bitcast.102), custom_call_target="tpu_custom_call" | custom-call | flops 402653184 | bytes 1572864 | tf_op jit(solution)/shard_map/cond/branch_4_fun/temporal_heads/pallas_call | solution.py:265
  103.1 31.6 %all_to_all.54 = bf16[64,8,384]{2,1,0:T(8,128)(2,1)S(1)} all-to-all(bf16[64,8,384]{2,1,0:T(8,128)(2,1)S(1)} %bitcast.63), channel_id=1, replica_groups=mesh['heads'=8,'frames'=64] {'frames'}, dimensions={0} | all-to-all | bytes 786432 | tf_op jit(solution)/shard_map/cond/branch_4_fun/all_to_all | solution.py:421
  134.7 0.7 merge_heads.10
  135.4 0.8 copy-done.19
  (10 shorter events, 0.0 us)
Async XLA Ops:
  2.5 12.1 %all-to-all-start.12 = ((f32[8,8,128]{2,1,0:T(8,128)}), f32[8,8,128]{2,1,0:T(8,128)S(1)}, u32[]{:S(2)}, u32[]{:S(2)}) async-start(f32[8,8,128]{2,1,0:T(8,128)} %square_sums.1), calls=%async_computation.12 | async-start | bytes 65536 | tf_op jit(solution)/shard_map/all_to_all | solution.py:412
  14.9 13.6 %copy-start.43 = (s32[5]{0:T(128)S(1)}, s32[5]{0:T(128)}, u32[]{:S(2)}) copy-start(s32[5]{0:T(128)} %get-tuple-element.197.kind_ref) | copy-start | bytes 64 | tf_op jit(solution)/shard_map/cond
  14.9 13.6 %copy-start.48 = (s32[5,4,12]{2,1,0:T(4,128)S(1)}, s32[5,4,12]{2,1,0:T(4,128)}, u32[]{:S(2)}) copy-start(s32[5,4,12]{2,1,0:T(4,128)} %get-tuple-element.282.mask_ref) | copy-start | bytes 2884 | tf_op jit(solution)/shard_map/cond
  15.0 13.6 %copy-start.54 = (s32[64]{0:T(128)S(1)}, s32[64]{0:T(128)}, u32[]{:S(2)}) copy-start(s32[64]{0:T(128)} %get-tuple-element.258) | copy-start | bytes 772 | tf_op jit(solution)/shard_map/cond
  17.1 17.9 %copy-start.6 = (bf16[512,640]{1,0:T(8,128)(2,1)S(1)}, bf16[512,640]{1,0:T(8,128)(2,1)}, u32[]{:S(2)}) copy-start(bf16[512,640]{1,0:T(8,128)(2,1)} %get-tuple-element.204.q_ref) | copy-start | bytes 1966084 | tf_op jit(solution)/shard_map/cond
  17.1 17.9 %copy-start.12 = (bf16[512,640]{1,0:T(8,128)(2,1)S(1)}, bf16[512,640]{1,0:T(8,128)(2,1)}, u32[]{:S(2)}) copy-start(bf16[512,640]{1,0:T(8,128)(2,1)} %get-tuple-element.205.k_ref) | copy-start | bytes 1966084 | tf_op jit(solution)/shard_map/cond
  17.1 17.9 %copy-start.14 = (bf16[1,512,640]{2,1,0:T(8,128)(2,1)S(1)}, bf16[1,512,640]{2,1,0:T(8,128)(2,1)}, u32[]{:S(2)}) copy-start(bf16[1,512,640]{2,1,0:T(8,128)(2,1)} %get-tuple-element.288) | copy-start | bytes 1966084 | tf_op jit(solution)/shard_map/cond
  17.2 17.9 %copy-start.31 = (f32[640]{0:T(1024)S(1)}, f32[640]{0:T(1024)}, u32[]{:S(2)}) copy-start(f32[640]{0:T(1024)} %get-tuple-element.264.gq_ref) | copy-start | bytes 7684 | tf_op jit(solution)/shard_map/cond
  17.2 17.9 %copy-start.37 = (f32[640]{0:T(1024)S(1)}, f32[640]{0:T(1024)}, u32[]{:S(2)}) copy-start(f32[640]{0:T(1024)} %get-tuple-element.270.gk_ref) | copy-start | bytes 7684 | tf_op jit(solution)/shard_map/cond
  17.2 7.5 %collective-permute-start.8 = (bf16[512,512]{1,0:T(8,128)(2,1)S(1)}, bf16[512,512]{1,0:T(8,128)(2,1)S(1)}, u32[]{:S(2)}, u32[]{:S(2)}) collective-permute-start(bf16[512,512]{1,0:T(8,128)(2,1)S(1)} %get-tuple-element.208.own_ref), channel_id=1, source_target_pairs={{0,1},{1,2},{2,3},{3,4},{4,5},{5,6},{6,7},{7,8},{8,9},{9,10},{10,1... | collective-permute-start | bytes 1572872 | tf_op jit(solution)/shard_map/cond/branch_4_fun/ppermute | solution.py:433
  18.6 9.9 %collective-permute-start.9 = (bf16[512,512]{1,0:T(8,128)(2,1)S(1)}, bf16[512,512]{1,0:T(8,128)(2,1)S(1)}, u32[]{:S(2)}, u32[]{:S(2)}) collective-permute-start(bf16[512,512]{1,0:T(8,128)(2,1)S(1)} %get-tuple-element.208.own_ref), channel_id=1, source_target_pairs={{1,0},{2,1},{3,2},{4,3},{5,4},{6,5},{7,6},{8,7},{9,8},{10,9},{11,1... | collective-permute-start | bytes 1572872 | tf_op jit(solution)/shard_map/cond/branch_4_fun/ppermute | solution.py:434
  135.4 0.8 copy-start.19

commit v5 on v4

--- a/solution.py
+++ b/solution.py
@@ -70,47 +70,73 @@
             flops=4 * q.size, bytes_accessed=4 * q.size, transcendentals=0
         ),
         name="square_sums",
-    )(q, k)
+    )(*(pltpu.with_memory_space_constraint(x, pltpu.HBM) for x in (q, k)))
+
+
+def stage_kernel(kind_ref, odd_ref, q_ref, k_ref, v_ref, staged_ref, choice_ref, sems):
+    heads, _, width = staged_ref.shape
+    size = width // 3
+
+    def copies(s):
+        columns = pl.ds(pl.multiple_of(head_at(s, kind_ref, heads) * size, size), size)
+        return [
+            pltpu.make_async_copy(
+                ref.at[:, columns],
+                staged_ref.at[s, :, pl.ds(n * size, size)],
+                sems.at[3 * s + n],
+            )
+            for n, ref in enumerate((q_ref, k_ref, v_ref))
+        ]
+
+    def begin(s, carry):
+        for copy in copies(s):
+            copy.start()
+        return carry
+
+    def end(s, carry):
+        for copy in copies(s):
+            copy.wait()
+        return carry
+
+    lax.fori_loop(0, heads, begin, 0)
+    count = sum(kind_ref[h] for h in range(heads))
+    second = (odd_ref[0] == 1) & (count > 2)
+    choice_ref[0] = count - 1 + jnp.where(second, heads - 3, 0)
+    lax.fori_loop(0, heads, end, 0)
+
+
+def stage(kind, odd, q, k, v):
+    tokens, channels = q.shape
+    heads = kind.shape[0]
+    return pl.pallas_call(
+        stage_kernel,
+        in_specs=[pl.BlockSpec(memory_space=pltpu.SMEM)] * 2
+        + [pl.BlockSpec(memory_space=pl.ANY)] * 3,
+        out_specs=[
+            pl.BlockSpec(memory_space=pltpu.VMEM),
+            pl.BlockSpec(memory_space=pltpu.SMEM),
+        ],
+        out_shape=[
+            pltpu.VMEM((heads, tokens, 3 * channels // heads), BF),
+            jax.ShapeDtypeStruct((1,), jnp.int32),
+        ],
+        scratch_shapes=[pltpu.SemaphoreType.DMA((3 * heads,))],
+        compiler_params=params(),
+        cost_estimate=pl.CostEstimate(flops=0, bytes_accessed=12 * q.size, transcendentals=0),
+        name="stage_heads",
+    )(kind, odd, *(pltpu.with_memory_space_constraint(x, pltpu.HBM) for x in (q, k, v)))
 
 
 def pack_kernel(
-    all_channels, tile, first, count, joined,
-    kind_ref, parts_ref, gq_ref, gk_ref, q_ref, k_ref, v_ref, *rest
+    all_channels, tile, first, count, joined, kind_ref, parts_ref, gq_ref, gk_ref, staged_ref, *rest
 ):
     if joined:
-        out_ref, q_buf, k_buf, out_buf, rq, rk, in_sems, out_sems = rest[-8:]
+        out_ref, out_buf, rq, rk, out_sems = rest[-5:]
     else:
-        out_ref, qn_ref, q_buf, k_buf, out_buf, rq, rk, in_sems, out_sems = rest[-9:]
-    tokens = q_ref.shape[0]
-    heads = kind_ref.shape[0]
-    size = q_ref.shape[1] // heads
+        out_ref, qn_ref, out_buf, rq, rk, out_sems = rest[-6:]
+    heads, tokens, _ = staged_ref.shape
     width = out_buf.shape[2]
-
-    def column(s):
-        return pl.multiple_of(head_at(first + s, kind_ref, heads) * size, size)
-
-    def loads(s):
-        columns = pl.ds(column(s), size)
-        trio = (
-            (q_ref, q_buf.at[s]),
-            (k_ref, k_buf.at[s]),
-            (v_ref, out_buf.at[s, :, pl.ds(width - size, size)]),
-        )
-        return [
-            pltpu.make_async_copy(ref.at[:, columns], buf, in_sems.at[3 * s + n])
-            for n, (ref, buf) in enumerate(trio)
-        ]
-
-    def stores(s):
-        columns = pl.ds(pl.multiple_of(s * width, width), width)
-        return pltpu.make_async_copy(out_buf.at[s], out_ref.at[:, columns], out_sems.at[s])
-
-    def begin(s, carry):
-        for copy in loads(s):
-            copy.start()
-        return carry
-
-    lax.fori_loop(0, count, begin, 0)
+    size = staged_ref.shape[2] // 3
     total = jnp.sum(parts_ref[...], axis=0)
     scale = lax.rsqrt(total / all_channels + epsilon)
     rows = tokens // tile
@@ -119,57 +145,57 @@
         rq[here, :] = jnp.broadcast_to(scale[c : c + 1, :], (tile, tile)).T
         rk[here, :] = jnp.broadcast_to(scale[rows + c : rows + c + 1, :], (tile, tile)).T
 
+    def store(s):
+        columns = pl.ds(pl.multiple_of(s * width, width), width)
+        return pltpu.make_async_copy(out_buf.at[s], out_ref.at[:, columns], out_sems.at[s])
+
     def work(s, carry):
-        gain_q = gq_ref[pl.ds(column(s), size)].reshape(1, size)
-        gain_k = gk_ref[pl.ds(column(s), size)].reshape(1, size)
-        copies = loads(s)
-        copies[0].wait()
-        normed_q = (q_buf[s].astype(F32) * rq[...] * gain_q).astype(BF)
-        copies[1].wait()
-        normed_k = (k_buf[s].astype(F32) * rk[...] * gain_k).astype(BF)
+        at = first + s
+        start = pl.multiple_of(head_at(at, kind_ref, heads) * size, size)
+        gain_q = gq_ref[pl.ds(start, size)].reshape(1, size)
+        gain_k = gk_ref[pl.ds(start, size)].reshape(1, size)
+        normed_q = (staged_ref[at, :, 0:size].astype(F32) * rq[...] * gain_q).astype(BF)
+        normed_k = (staged_ref[at, :, size : 2 * size].astype(F32) * rk[...] * gain_k).astype(BF)
         if joined:
             out_buf[s, :, 0:size] = normed_q
-            out_buf[s, :, size : 2 * size] = normed_k
         else:
-            columns = pl.ds(pl.multiple_of(s * size, size), size)
-            qn_ref[:, columns] = normed_q
-            out_buf[s, :, 0:size] = normed_k
-        copies[2].wait()
-        stores(s).start()
+            qn_ref[:, pl.ds(pl.multiple_of(s * size, size), size)] = normed_q
+        out_buf[s, :, width - 2 * size : width - size] = normed_k
+        out_buf[s, :, width - size : width] = staged_ref[at, :, 2 * size : 3 * size]
+        store(s).start()
         return carry
 
     lax.fori_loop(0, count, work, 0)
 
     def end(s, carry):
-        stores(s).wait()
+        store(s).wait()
         return carry
 
     lax.fori_loop(0, count, end, 0)
 
 
-def pack(kind, parts, gain_q, gain_k, q, k, v, after, first, count, joined, all_channels, tile):
-    tokens, channels = q.shape
-    size = channels // kind.shape[0]
+def pack(kind, parts, gain_q, gain_k, staged, after, first, count, joined, all_channels, tile):
+    _, tokens, wide = staged.shape
+    size = wide // 3
     width = (3 if joined else 2) * size
     out_shape = [jax.ShapeDtypeStruct((tokens, count * width), BF)]
     out_specs = [pl.BlockSpec(memory_space=pl.ANY)]
+    if joined:
+        out_shape = [pltpu.HBM((tokens, count * width), BF)]
     if not joined:
         out_shape.append(jax.ShapeDtypeStruct((tokens, count * size), BF))
         out_specs.append(pl.BlockSpec(memory_space=pltpu.VMEM))
     return pl.pallas_call(
         functools.partial(pack_kernel, all_channels, tile, first, count, joined),
         in_specs=[pl.BlockSpec(memory_space=pltpu.SMEM)]
-        + [pl.BlockSpec(memory_space=pltpu.VMEM)] * 3
-        + [pl.BlockSpec(memory_space=pl.ANY)] * (3 + len(after)),
+        + [pl.BlockSpec(memory_space=pltpu.VMEM)] * 4
+        + [pl.BlockSpec(memory_space=pl.ANY)] * len(after),
         out_specs=out_specs,
         out_shape=out_shape,
         scratch_shapes=[
-            pltpu.VMEM((count, tokens, size), BF),
-            pltpu.VMEM((count, tokens, size), BF),
             pltpu.VMEM((count, tokens, width), BF),
             pltpu.VMEM((tokens, size), F32),
             pltpu.VMEM((tokens, size), F32),
-            pltpu.SemaphoreType.DMA((3 * count,)),
             pltpu.SemaphoreType.DMA((count,)),
         ],
         compiler_params=params(),
@@ -179,7 +205,7 @@
             transcendentals=0,
         ),
         name="pack_temporal" if joined else "pack_spatial",
-    )(kind, parts, gain_q, gain_k, q, k, v, *after)
+    )(kind, parts, gain_q, gain_k, staged, *after)
 
 
 def video_rows(frames, share):
@@ -408,7 +434,9 @@
     share = tokens // frames
     q, k, v = queries[0], keys[0], values[0]
 
+    odd = lax.axis_index("heads") % 2
     parts = local_sums(q, k, blocks, tile)
+    staged, choice = stage(head_kind, odd[None], q, k, v)
     parts = lax.all_to_all(parts, "heads", split_axis=0, concat_axis=0, tiled=True)
 
     place = position[None]
@@ -425,8 +453,8 @@
     def branch(count, late):
         rest = heads - count
 
-        def run(q, k, v, parts):
-            args = (head_kind, parts, gain_q, gain_k, q, k, v)
+        def run(staged, parts):
+            args = (head_kind, parts, gain_q, gain_k, staged)
 
             def near():
                 pair, near_q = pack(*args, (), count, rest, False, blocks * channels, tile)
@@ -465,12 +493,9 @@
 
         return run
 
-    count = jnp.sum(head_kind)
-    odd = lax.axis_index("heads") % 2
-    choice = count - 1 + jnp.where((odd == 1) & (count > 2), heads - 3, 0)
     branches = [branch(c, 0) for c in range(1, heads)]
     branches += [branch(c, 2) for c in range(3, heads)]
-    out = lax.switch(choice, branches, q, k, v, parts)
+    out = lax.switch(choice[0], branches, staged, parts)
     return out[None]
 
 

time: 137 us -> 149 us (1.088)
  the two profiles are of different devices: /device:TPU:5 before, /device:TPU:1 now
where the time goes in v5:
time: 149 us
  blocking collectives  111 us (74%)
  Pallas kernels  16.7 us (11%)
  starting transfers between devices  12.7 us (9%)
  waiting for transfers between devices  6.96 us (5%)
    all_to_all x2, blocking collectives, exchange(): lax.all_to_all(x, 'frames', split_axis=0, concat_axis=0, tiled=True)  111 us
    all_to_all x1, starting transfers between devices, local(): lax.all_to_all(parts, 'heads', split_axis=0, concat_axis=0, tiled=True)  10.1 us
    pallas_call x1, Pallas kernels, spatial(): pl.pallas_call(functools.partial(spatial_kernel, scale, tile, first), gri...  3.88 us
    ppermute x1, waiting for transfers between devices, near(): later = lax.ppermute(pair, 'frames', down)  3.83 us
    pallas_call x1, Pallas kernels, temporal(): pl.pallas_call(functools.partial(temporal_kernel, scale, count, share), i...  3.02 us
  transfers between devices with their start and end apart: 3, of which 3 were waited for; matrix products, arithmetic and copies ran while one was open for 0% of the time, Pallas kernels for 2%

profile of v5, /device:TPU:1, one launch (start us, length us, event | category | flops | bytes accessed | tf_op | source)
XLA Modules:
  0.0 149.2 jit_solution(14439736596790722705)
XLA Ops:
  0.0 0.0 copy-start.14
  0.0 0.0 copy-start.17
  0.0 0.0 copy-start.22
  0.0 2.6 %square_sums.1 = f32[8,8,128]{2,1,0:T(8,128)} custom-call(bf16[512,640]{1,0:T(8,128)(2,1)} %bitcast.66, bf16[512,640]{1,0:T(8,128)(2,1)} %bitcast.68), custom_call_target="tpu_custom_call" | custom-call | flops 1310720 | bytes 1310720 | tf_op jit(solution)/shard_map/square_sums/pallas_call | solution.py:61
  2.6 10.1 %all-to-all-start.12 = ((f32[8,8,128]{2,1,0:T(8,128)}), f32[8,8,128]{2,1,0:T(8,128)S(1)}, u32[]{:S(2)}, u32[]{:S(2)}) async-start(f32[8,8,128]{2,1,0:T(8,128)} %square_sums.1), calls=%async_computation.12 | async-start | bytes 65536 | tf_op jit(solution)/shard_map/all_to_all | solution.py:440
  12.8 3.0 %stage_heads.1 = (bf16[5,512,384]{2,1,0:T(8,128)(2,1)S(1)}, s32[1]{0:T(128)}) custom-call(s32[5]{0:T(128)} %kind_ref.1, s32[1]{0:T(128)} %bitcast.42.odd_ref, bf16[512,640]{1,0:T(8,128)(2,1)} %bitcast.67, bf16[512,640]{1,0:T(8,128)(2,1)} %bitcast.69, bf16[512,640]{1,0:T(8,128)(2,1)} %bitcast.71), custom_call_target="tpu_custom_call" | custom-call | bytes 3932160 | tf_op jit(solution)/shard_map/stage_heads/pallas_call | solution.py:111
  16.3 1.1 all-to-all-done.12
  17.5 0.0 copy-done.14
  17.5 0.0 copy-done.15
  17.5 0.0 copy-done.16
  17.5 0.0 copy-done.17
  17.5 0.0 copy-done.22
  17.5 131.4 %conditional.1 = (bf16[1,512,640]{2,1,0:T(8,128)(2,1)}) conditional(s32[]{:T(128)} %bitcast.46, (s32[5]{0:T(128)S(1)}, f32[8,8,128]{2,1,0:T(8,128)S(1)}, f32[640]{0:T(1024)S(1)}, f32[640]{0:T(1024)S(1)}, bf16[5,512,384]{2,1,0:T(8,128)(2,1)S(1)}, /*index=5*/s32[5,4,12]{2,1,0:T(4,128)S(1)}, s32[64]{0:T(128)S(1)}, ...), branch_computations={%region_0.1_spmd, %region_1.2_spmd, %region_2.3_spmd, %region_3.4_... | conditional | flops 1746141184 | bytes 23593196 | solution.py:498
  17.8 0.8 pack_spatial.11
  18.6 1.3 collective-permute-start.10
  19.9 1.3 collective-permute-start.11
  21.2 2.0 %collective-permute-done.10.before_ref = bf16[512,256]{1,0:T(8,128)(2,1)S(1)} collective-permute-done((bf16[512,256]{1,0:T(8,128)(2,1)S(1)}, bf16[512,256]{1,0:T(8,128)(2,1)S(1)}, u32[]{:S(2)}, u32[]{:S(2)}) %collective-permute-start.10) | collective-permute-done | bytes 262176 | tf_op jit(solution)/shard_map/cond/branch_5_fun/ppermute | solution.py:461
  23.2 3.8 %collective-permute-done.11.after_ref = bf16[512,256]{1,0:T(8,128)(2,1)S(1)} collective-permute-done((bf16[512,256]{1,0:T(8,128)(2,1)S(1)}, bf16[512,256]{1,0:T(8,128)(2,1)S(1)}, u32[]{:S(2)}, u32[]{:S(2)}) %collective-permute-start.11) | collective-permute-done | bytes 262176 | tf_op jit(solution)/shard_map/cond/branch_5_fun/ppermute | solution.py:462
  27.0 3.9 %spatial_heads.11.rest_0_.base_ref = bf16[512,640]{1,0:T(8,128)(2,1)} custom-call(s32[5]{0:T(128)S(1)} %get-tuple-element.176.kind_ref, s32[5,4,12]{2,1,0:T(4,128)S(1)} %get-tuple-element.239.mask_ref, s32[64]{0:T(128)S(1)} %get-tuple-element.221, s32[1]{0:T(128)} %bitcast.35.place_ref, bf16[512,128]{1,0:T(8,128)(2,1)S(1)} %get-tuple-element.184.q_ref, ...), custom_call_target="tpu_custom_call" | custom-call | flops 402653184 | bytes 1048576 | tf_op jit(solution)/shard_map/cond/branch_5_fun/spatial_heads/pallas_call | solution.py:372
  30.9 2.1 %pack_temporal.11 = bf16[512,1536]{1,0:T(8,128)(2,1)} custom-call(s32[5]{0:T(128)S(1)} %get-tuple-element.176.kind_ref, f32[8,8,128]{2,1,0:T(8,128)S(1)} %get-tuple-element.180.parts_ref, f32[640]{0:T(1024)S(1)} %get-tuple-element.227.gq_ref, f32[640]{0:T(1024)S(1)} %get-tuple-element.233.gk_ref, bf16[5,512,384]{2,1,0:T(8,128)(2,1)S(1)} %get-tuple-element.183.staged_ref, ...), custom_call_target="tpu_custom_call" | custom-call | flops 1048576 | bytes 3145728 | tf_op jit(solution)/shard_map/cond/branch_5_fun/pack_temporal/pallas_call | solution.py:188
  33.0 77.9 %all_to_all.55 = bf16[64,8,1536]{2,1,0:T(8,128)(2,1)S(1)} all-to-all(bf16[64,8,1536]{2,1,0:T(8,128)(2,1)} %bitcast.61), channel_id=1, replica_groups=mesh['heads'=8,'frames'=64] {'frames'}, dimensions={0} | all-to-all | bytes 3145728 | tf_op jit(solution)/shard_map/cond/branch_5_fun/all_to_all | solution.py:449
  110.9 3.0 %temporal_heads.11 = bf16[512,512]{1,0:T(8,128)(2,1)S(1)} custom-call(bf16[512,1536]{1,0:T(8,128)(2,1)S(1)} %bitcast.48, s32[1,64]{1,0:T(1,128)S(1)} %bitcast.77), custom_call_target="tpu_custom_call" | custom-call | flops 536870912 | bytes 2097152 | tf_op jit(solution)/shard_map/cond/branch_5_fun/temporal_heads/pallas_call | solution.py:291
  113.9 33.3 %all_to_all.56 = bf16[64,8,512]{2,1,0:T(8,128)(2,1)S(1)} all-to-all(bf16[64,8,512]{2,1,0:T(8,128)(2,1)S(1)} %bitcast.52), channel_id=1, replica_groups=mesh['heads'=8,'frames'=64] {'frames'}, dimensions={0} | all-to-all | bytes 1048576 | tf_op jit(solution)/shard_map/cond/branch_5_fun/all_to_all | solution.py:449
  147.3 1.4 merge_heads.11
  (2 shorter events, 0.0 us)
Async XLA Ops:
  0.0 17.5 %copy-start.14 = (f32[640]{0:T(1024)S(1)}, f32[640]{0:T(1024)}, u32[]{:S(2)}) copy-start(f32[640]{0:T(1024)} %param.17) | copy-start | bytes 7684
  0.0 17.5 %copy-start.15 = (f32[640]{0:T(1024)S(1)}, f32[640]{0:T(1024)}, u32[]{:S(2)}) copy-start(f32[640]{0:T(1024)} %param.18) | copy-start | bytes 7684
  0.0 17.5 %copy-start.16 = (s32[5]{0:T(128)S(1)}, s32[5]{0:T(128)}, u32[]{:S(2)}) copy-start(s32[5]{0:T(128)} %kind_ref.1) | copy-start | bytes 64
  0.0 17.5 %copy-start.17 = (s32[5,4,12]{2,1,0:T(4,128)S(1)}, s32[5,4,12]{2,1,0:T(4,128)}, u32[]{:S(2)}) copy-start(s32[5,4,12]{2,1,0:T(4,128)} %param.20) | copy-start | bytes 2884
  0.0 17.5 %copy-start.22 = (s32[64]{0:T(128)S(1)}, s32[64]{0:T(128)}, u32[]{:S(2)}) copy-start(s32[64]{0:T(128)} %param.21) | copy-start | bytes 772
  2.6 14.9 %all-to-all-start.12 = ((f32[8,8,128]{2,1,0:T(8,128)}), f32[8,8,128]{2,1,0:T(8,128)S(1)}, u32[]{:S(2)}, u32[]{:S(2)}) async-start(f32[8,8,128]{2,1,0:T(8,128)} %square_sums.1), calls=%async_computation.12 | async-start | bytes 65536 | tf_op jit(solution)/shard_map/all_to_all | solution.py:440
  18.6 4.6 %collective-permute-start.10 = (bf16[512,256]{1,0:T(8,128)(2,1)S(1)}, bf16[512,256]{1,0:T(8,128)(2,1)S(1)}, u32[]{:S(2)}, u32[]{:S(2)}) collective-permute-start(bf16[512,256]{1,0:T(8,128)(2,1)S(1)} %get-tuple-element.185.own_ref), channel_id=1, source_target_pairs={{0,1},{1,2},{2,3},{3,4},{4,5},{5,6},{6,7},{7,8},{8,9},{9,10},{10,1... | collective-permute-start | bytes 786440 | tf_op jit(solution)/shard_map/cond/branch_5_fun/ppermute | solution.py:461
  19.9 7.1 %collective-permute-start.11 = (bf16[512,256]{1,0:T(8,128)(2,1)S(1)}, bf16[512,256]{1,0:T(8,128)(2,1)S(1)}, u32[]{:S(2)}, u32[]{:S(2)}) collective-permute-start(bf16[512,256]{1,0:T(8,128)(2,1)S(1)} %get-tuple-element.185.own_ref), channel_id=1, source_target_pairs={{1,0},{2,1},{3,2},{4,3},{5,4},{6,5},{7,6},{8,7},{9,8},{10,9},{11,1... | collective-permute-start | bytes 786440 | tf_op jit(solution)/shard_map/cond/branch_5_fun/ppermute | solution.py:462

commit v6 on v5

--- a/solution.py
+++ b/solution.py
@@ -325,7 +325,6 @@
     heads = kind_ref.shape[0]
     head = head_at(first + pl.program_id(0), kind_ref, heads)
     tiles = own_ref.shape[0] // tile
-    i = pl.program_id(1)
     frames = (before_ref, own_ref, after_ref)
     place = place_ref[0]
     last = valid_ref.shape[0] - 1
@@ -334,34 +333,40 @@
         same = ((there + SHIFT) // VIDEO == (place + SHIFT) // VIDEO) & (there != place)
         near[o] = same & (valid_ref[there] > 0)
     own_live = jnp.where(valid_ref[place] > 0, 1.0, 0.0).astype(F32)
-    q = q_ref[...]
-    pieces = []
-    for o in range(3):
-        s = lax.dot_general(
-            q, frames[o][:, 0:128], (((1,), (1,)), ((), ())), preferred_element_type=F32
-        )
-        for j in range(tiles):
-            ok = (mask_ref[head, i, o * tiles + j] > 0) & near[o]
-            low = jnp.where(ok, 0.0, LOW).astype(F32)
-            pieces.append(s[:, j * tile : (j + 1) * tile] + low)
-    top = pieces[0]
-    for x in pieces[1:]:
-        top = jnp.maximum(top, x)
-    top = jnp.max(top, axis=1, keepdims=True)
-    pieces = [jnp.exp2((x - top) * scale) for x in pieces]
-    total = pieces[0]
-    for x in pieces[1:]:
-        total = total + x
-    total = jnp.sum(total, axis=1, keepdims=True)
-    o_sum = None
-    for o in range(3):
-        p = jnp.concatenate([x.astype(BF) for x in pieces[o * tiles : (o + 1) * tiles]], axis=1)
-        part = jnp.dot(p, frames[o][:, 128:256], preferred_element_type=F32)
-        o_sum = part if o_sum is None else o_sum + part
-    out_ref[...] = (o_sum / total * own_live).astype(BF)
-
-
-def spatial(kind, mask, valid, place, q, own, before, after, first, count, channels, scale, tile):
+    parts = q_ref.shape[0] // tile
+    for sub in range(parts):
+        i = pl.program_id(1) * parts + sub
+        rows = pl.ds(sub * tile, tile)
+        q = q_ref[rows, :]
+        pieces = []
+        for o in range(3):
+            s = lax.dot_general(
+                q, frames[o][:, 0:128], (((1,), (1,)), ((), ())), preferred_element_type=F32
+            )
+            for j in range(tiles):
+                ok = (mask_ref[head, i, o * tiles + j] > 0) & near[o]
+                low = jnp.where(ok, 0.0, LOW).astype(F32)
+                pieces.append(s[:, j * tile : (j + 1) * tile] + low)
+        top = pieces[0]
+        for x in pieces[1:]:
+            top = jnp.maximum(top, x)
+        top = jnp.max(top, axis=1, keepdims=True)
+        pieces = [jnp.exp2((x - top) * scale) for x in pieces]
+        total = pieces[0]
+        for x in pieces[1:]:
+            total = total + x
+        total = jnp.sum(total, axis=1, keepdims=True)
+        o_sum = None
+        for o in range(3):
+            p = jnp.concatenate([x.astype(BF) for x in pieces[o * tiles : (o + 1) * tiles]], axis=1)
+            part = jnp.dot(p, frames[o][:, 128:256], preferred_element_type=F32)
+            o_sum = part if o_sum is None else o_sum + part
+        out_ref[rows, :] = (o_sum / total * own_live).astype(BF)
+
+
+def spatial(
+    kind, mask, valid, place, q, own, before, after, first, count, channels, scale, tile, step
+):
     tokens = q.shape[0]
     heads = kind.shape[0]
     size = channels // heads
@@ -373,11 +378,11 @@
         functools.partial(spatial_kernel, scale, tile, first),
         grid_spec=pltpu.PrefetchScalarGridSpec(
             num_scalar_prefetch=4,
-            grid=(count, tokens // tile),
-            in_specs=[pl.BlockSpec((tile, size), lambda i, j, *_: (j, i))]
+            grid=(count, tokens // step),
+            in_specs=[pl.BlockSpec((step, size), lambda i, j, *_: (j, i))]
             + [pl.BlockSpec((tokens, 2 * size), slot)] * 3,
             out_specs=pl.BlockSpec(
-                (tile, size),
+                (step, size),
                 lambda i, j, kind_ref, *_: (j, head_at(first + i, kind_ref, heads)),
             ),
         ),
@@ -465,7 +470,7 @@
             def attend(near_q, pair, earlier, later):
                 return spatial(
                     head_kind, tile_mask, frame_valid, place, near_q, pair, earlier, later,
-                    count, rest, channels, scale, tile,
+                    count, rest, channels, scale, tile, tile if late == 2 else 2 * tile,
                 )
 
             def send(*after):

time: 149 us -> 150 us (level)
  no operation moved by 1% of the time
where the time goes in v6:
time: 150 us; the launch traced here: 149 us
  blocking collectives  111 us (74%)
  Pallas kernels  16.7 us (11%)
  starting transfers between devices  12.7 us (8%)
  waiting for transfers between devices  6.96 us (5%)
    all_to_all x2, blocking collectives, exchange(): lax.all_to_all(x, 'frames', split_axis=0, concat_axis=0, tiled=True)  111 us
    all_to_all x1, starting transfers between devices, local(): lax.all_to_all(parts, 'heads', split_axis=0, concat_axis=0, tiled=True)  10.1 us
    pallas_call x1, Pallas kernels, spatial(): pl.pallas_call(functools.partial(spatial_kernel, scale, tile, first), gri...  3.88 us
    ppermute x1, waiting for transfers between devices, near(): later = lax.ppermute(pair, 'frames', down)  3.83 us
    pallas_call x1, Pallas kernels, temporal(): pl.pallas_call(functools.partial(temporal_kernel, scale, count, share), i...  3.02 us
  transfers between devices with their start and end apart: 3, of which 3 were waited for; matrix products, arithmetic and copies ran while one was open for 0% of the time, Pallas kernels for 2%

profile of v6, /device:TPU:1, one launch (start us, length us, event | category | flops | bytes accessed | tf_op | source)
XLA Modules:
  0.0 149.2 jit_solution(6128154582493959316)
XLA Ops:
  0.0 0.0 copy-start.14
  0.0 0.0 copy-start.17
  0.0 0.0 copy-start.22
  0.0 2.6 %square_sums.1 = f32[8,8,128]{2,1,0:T(8,128)} custom-call(bf16[512,640]{1,0:T(8,128)(2,1)} %bitcast.66, bf16[512,640]{1,0:T(8,128)(2,1)} %bitcast.68), custom_call_target="tpu_custom_call" | custom-call | flops 1310720 | bytes 1310720 | tf_op jit(solution)/shard_map/square_sums/pallas_call | solution.py:61
  2.6 10.1 %all-to-all-start.12 = ((f32[8,8,128]{2,1,0:T(8,128)}), f32[8,8,128]{2,1,0:T(8,128)S(1)}, u32[]{:S(2)}, u32[]{:S(2)}) async-start(f32[8,8,128]{2,1,0:T(8,128)} %square_sums.1), calls=%async_computation.12 | async-start | bytes 65536 | tf_op jit(solution)/shard_map/all_to_all | solution.py:445
  12.8 3.0 %stage_heads.1 = (bf16[5,512,384]{2,1,0:T(8,128)(2,1)S(1)}, s32[1]{0:T(128)}) custom-call(s32[5]{0:T(128)} %kind_ref.1, s32[1]{0:T(128)} %bitcast.42.odd_ref, bf16[512,640]{1,0:T(8,128)(2,1)} %bitcast.67, bf16[512,640]{1,0:T(8,128)(2,1)} %bitcast.69, bf16[512,640]{1,0:T(8,128)(2,1)} %bitcast.71), custom_call_target="tpu_custom_call" | custom-call | bytes 3932160 | tf_op jit(solution)/shard_map/stage_heads/pallas_call | solution.py:111
  16.3 1.1 all-to-all-done.12
  17.5 0.0 copy-done.14
  17.5 0.0 copy-done.15
  17.5 0.0 copy-done.16
  17.5 0.0 copy-done.17
  17.5 0.0 copy-done.22
  17.5 131.4 %conditional.1 = (bf16[1,512,640]{2,1,0:T(8,128)(2,1)}) conditional(s32[]{:T(128)} %bitcast.46, (s32[5]{0:T(128)S(1)}, f32[8,8,128]{2,1,0:T(8,128)S(1)}, f32[640]{0:T(1024)S(1)}, f32[640]{0:T(1024)S(1)}, bf16[5,512,384]{2,1,0:T(8,128)(2,1)S(1)}, /*index=5*/s32[5,4,12]{2,1,0:T(4,128)S(1)}, s32[64]{0:T(128)S(1)}, ...), branch_computations={%region_0.1_spmd, %region_1.2_spmd, %region_2.3_spmd, %region_3.4_... | conditional | flops 1746141184 | bytes 23593196 | solution.py:503
  17.8 0.8 pack_spatial.11
  18.6 1.3 collective-permute-start.10
  19.9 1.3 collective-permute-start.11
  21.2 2.0 %collective-permute-done.10.before_ref = bf16[512,256]{1,0:T(8,128)(2,1)S(1)} collective-permute-done((bf16[512,256]{1,0:T(8,128)(2,1)S(1)}, bf16[512,256]{1,0:T(8,128)(2,1)S(1)}, u32[]{:S(2)}, u32[]{:S(2)}) %collective-permute-start.10) | collective-permute-done | bytes 262176 | tf_op jit(solution)/shard_map/cond/branch_5_fun/ppermute | solution.py:466
  23.2 3.8 %collective-permute-done.11.after_ref = bf16[512,256]{1,0:T(8,128)(2,1)S(1)} collective-permute-done((bf16[512,256]{1,0:T(8,128)(2,1)S(1)}, bf16[512,256]{1,0:T(8,128)(2,1)S(1)}, u32[]{:S(2)}, u32[]{:S(2)}) %collective-permute-start.11) | collective-permute-done | bytes 262176 | tf_op jit(solution)/shard_map/cond/branch_5_fun/ppermute | solution.py:467
  27.0 3.9 %spatial_heads.11.rest_0_.base_ref = bf16[512,640]{1,0:T(8,128)(2,1)} custom-call(s32[5]{0:T(128)S(1)} %get-tuple-element.176.kind_ref, s32[5,4,12]{2,1,0:T(4,128)S(1)} %get-tuple-element.239.mask_ref, s32[64]{0:T(128)S(1)} %get-tuple-element.221, s32[1]{0:T(128)} %bitcast.35.place_ref, bf16[512,128]{1,0:T(8,128)(2,1)S(1)} %get-tuple-element.184.q_ref, ...), custom_call_target="tpu_custom_call" | custom-call | flops 402653184 | bytes 1048576 | tf_op jit(solution)/shard_map/cond/branch_5_fun/spatial_heads/pallas_call | solution.py:377
  30.9 2.1 %pack_temporal.11 = bf16[512,1536]{1,0:T(8,128)(2,1)} custom-call(s32[5]{0:T(128)S(1)} %get-tuple-element.176.kind_ref, f32[8,8,128]{2,1,0:T(8,128)S(1)} %get-tuple-element.180.parts_ref, f32[640]{0:T(1024)S(1)} %get-tuple-element.227.gq_ref, f32[640]{0:T(1024)S(1)} %get-tuple-element.233.gk_ref, bf16[5,512,384]{2,1,0:T(8,128)(2,1)S(1)} %get-tuple-element.183.staged_ref, ...), custom_call_target="tpu_custom_call" | custom-call | flops 1048576 | bytes 3145728 | tf_op jit(solution)/shard_map/cond/branch_5_fun/pack_temporal/pallas_call | solution.py:188
  33.0 77.9 %all_to_all.55 = bf16[64,8,1536]{2,1,0:T(8,128)(2,1)S(1)} all-to-all(bf16[64,8,1536]{2,1,0:T(8,128)(2,1)} %bitcast.61), channel_id=1, replica_groups=mesh['heads'=8,'frames'=64] {'frames'}, dimensions={0} | all-to-all | bytes 3145728 | tf_op jit(solution)/shard_map/cond/branch_5_fun/all_to_all | solution.py:454
  110.9 3.0 %temporal_heads.11 = bf16[512,512]{1,0:T(8,128)(2,1)S(1)} custom-call(bf16[512,1536]{1,0:T(8,128)(2,1)S(1)} %bitcast.48, s32[1,64]{1,0:T(1,128)S(1)} %bitcast.77), custom_call_target="tpu_custom_call" | custom-call | flops 536870912 | bytes 2097152 | tf_op jit(solution)/shard_map/cond/branch_5_fun/temporal_heads/pallas_call | solution.py:291
  113.9 33.3 %all_to_all.56 = bf16[64,8,512]{2,1,0:T(8,128)(2,1)S(1)} all-to-all(bf16[64,8,512]{2,1,0:T(8,128)(2,1)S(1)} %bitcast.52), channel_id=1, replica_groups=mesh['heads'=8,'frames'=64] {'frames'}, dimensions={0} | all-to-all | bytes 1048576 | tf_op jit(solution)/shard_map/cond/branch_5_fun/all_to_all | solution.py:454
  147.3 1.4 merge_heads.11
  (2 shorter events, 0.0 us)
Async XLA Ops:
  0.0 17.5 %copy-start.14 = (f32[640]{0:T(1024)S(1)}, f32[640]{0:T(1024)}, u32[]{:S(2)}) copy-start(f32[640]{0:T(1024)} %param.17) | copy-start | bytes 7684
  0.0 17.5 %copy-start.15 = (f32[640]{0:T(1024)S(1)}, f32[640]{0:T(1024)}, u32[]{:S(2)}) copy-start(f32[640]{0:T(1024)} %param.18) | copy-start | bytes 7684
  0.0 17.5 %copy-start.16 = (s32[5]{0:T(128)S(1)}, s32[5]{0:T(128)}, u32[]{:S(2)}) copy-start(s32[5]{0:T(128)} %kind_ref.1) | copy-start | bytes 64
  0.0 17.5 %copy-start.17 = (s32[5,4,12]{2,1,0:T(4,128)S(1)}, s32[5,4,12]{2,1,0:T(4,128)}, u32[]{:S(2)}) copy-start(s32[5,4,12]{2,1,0:T(4,128)} %param.20) | copy-start | bytes 2884
  0.0 17.5 %copy-start.22 = (s32[64]{0:T(128)S(1)}, s32[64]{0:T(128)}, u32[]{:S(2)}) copy-start(s32[64]{0:T(128)} %param.21) | copy-start | bytes 772
  2.6 14.9 %all-to-all-start.12 = ((f32[8,8,128]{2,1,0:T(8,128)}), f32[8,8,128]{2,1,0:T(8,128)S(1)}, u32[]{:S(2)}, u32[]{:S(2)}) async-start(f32[8,8,128]{2,1,0:T(8,128)} %square_sums.1), calls=%async_computation.12 | async-start | bytes 65536 | tf_op jit(solution)/shard_map/all_to_all | solution.py:445
  18.6 4.6 %collective-permute-start.10 = (bf16[512,256]{1,0:T(8,128)(2,1)S(1)}, bf16[512,256]{1,0:T(8,128)(2,1)S(1)}, u32[]{:S(2)}, u32[]{:S(2)}) collective-permute-start(bf16[512,256]{1,0:T(8,128)(2,1)S(1)} %get-tuple-element.185.own_ref), channel_id=1, source_target_pairs={{0,1},{1,2},{2,3},{3,4},{4,5},{5,6},{6,7},{7,8},{8,9},{9,10},{10,1... | collective-permute-start | bytes 786440 | tf_op jit(solution)/shard_map/cond/branch_5_fun/ppermute | solution.py:466
  19.9 7.1 %collective-permute-start.11 = (bf16[512,256]{1,0:T(8,128)(2,1)S(1)}, bf16[512,256]{1,0:T(8,128)(2,1)S(1)}, u32[]{:S(2)}, u32[]{:S(2)}) collective-permute-start(bf16[512,256]{1,0:T(8,128)(2,1)S(1)} %get-tuple-element.185.own_ref), channel_id=1, source_target_pairs={{1,0},{2,1},{3,2},{4,3},{5,4},{6,5},{7,6},{8,7},{9,8},{10,9},{11,1... | collective-permute-start | bytes 786440 | tf_op jit(solution)/shard_map/cond/branch_5_fun/ppermute | solution.py:467
